TPU v7x, 512 devices: a whole 4x8x8 slice. The times are simulated.
512 devices in a mesh: inst: 32 (over x, z), head: 16 (over y, core).
Axes of the slice: x: 4, y: 8, z: 8, core: 2. Of those that a mesh axis runs over, the one named last changes fastest.
Arguments:
- hidden_rows: bfloat16 [32, 32, 16, 9216], P('inst', None, None, 'head'), may hold values from -6 to 6
- send_counts: int32 [32, 32], P('inst'), may hold values from 0 to 16, as said below
- row_session: int32 [32, 32, 16], P('inst'), may hold values from 0 to 1, as said below
- row_position: int32 [32, 32, 16], P('inst'), may hold values from 0 to 1023, as said below
- resident_lengths: int32 [64], P('inst'), may hold values from 1 to 512, as said below
- kv_weight: bfloat16 [9216, 12288], P('inst', 'head'), may hold values from -0.0625 to 0.0625
- key_cache: bfloat16 [64, 1024, 6144], P('inst', None, 'head'), as said below
- value_cache: bfloat16 [64, 1024, 6144], P('inst', None, 'head'), may hold values from -6 to 6
- query: bfloat16 [64, 6144], P('inst', 'head'), as said below
- new_key: bfloat16 [64, 6144], P('inst', 'head'), may hold values from -6 to 6
- new_value: bfloat16 [64, 6144], P('inst', 'head'), may hold values from -6 to 6
Outputs:
- attended: bfloat16 [64, 6144], P('inst', 'head')
Inputs may be any that keep to these rules, and one draw needn't show every extreme that they name: `send_counts`: at most 16 live slots from one source to one destination; in every draw one destination instance receives 16 rows from every source. `row_session`: for a live slot, a session of the destination instance; 0 in slots that are not live. The destination that receives 16 rows from every source sends all of them to one of its sessions. `row_position`: the live rows of one destination session take each of the positions from its resident length to its resident length plus their number minus 1 exactly once; 0 in slots that are not live. In every draw some session's rows end at position 1023. `resident_lengths`: A session's resident length plus its restored rows stays within 1024 positions. `key_cache`: entries of order one. `query`: entries of order one or a few tens.
All inputs are finite; a program needn't handle non-finite values.
Results may differ from a plain program's by a relative error of at most 0.009.
Values may be sent and summed in bfloat16 or wider, within the bound.
No kernel may reach another device: no remote copies, remote signals or barrier semaphores. Data moves between devices by JAX's collectives and lax.ppermute only.
A program may use at most 192 MiB of HBM per device.

v0:
```python
import math

import jax
import jax.numpy as jnp
from jax import lax
from jax.sharding import PartitionSpec as P

HDIM = 128


masked_score = -1e30


def local(
    hidden_rows,
    send_counts,
    row_session,
    row_position,
    resident_lengths,
    kv_weight,
    key_cache,
    value_cache,
    query,
    new_key,
    new_value,
):
    sources = hidden_rows.shape[1]
    slot_cap = hidden_rows.shape[2]
    slot_count = sources * slot_cap
    head_dev = query.shape[1] // HDIM
    sessions_dev = key_cache.shape[0]
    context = key_cache.shape[1]
    inverse_root = 1.0 / math.sqrt(HDIM)
    arrived, counts_in, session_in, position_in = (
        lax.all_to_all(hidden_rows, "inst", split_axis=1, concat_axis=0, tiled=True),
        lax.all_to_all(send_counts, "inst", split_axis=1, concat_axis=0, tiled=True),
        lax.all_to_all(row_session, "inst", split_axis=1, concat_axis=0, tiled=True),
        lax.all_to_all(row_position, "inst", split_axis=1, concat_axis=0, tiled=True),
    )
    full_rows = lax.all_gather(
        arrived.reshape(slot_count, arrived.shape[3]), "head", axis=1, tiled=True
    )
    restored = jnp.dot(
        full_rows,
        lax.all_gather(kv_weight, "inst", axis=0, tiled=True),
        preferred_element_type=jnp.float32,
    )
    restored = restored.astype(jnp.bfloat16).reshape(slot_count, head_dev, 2, HDIM)
    restored_keys = restored[:, :, 0]
    restored_values = restored[:, :, 1]
    slot_live = (jnp.arange(slot_cap)[None, :] < counts_in).reshape(slot_count)
    session_map = session_in.reshape(slot_count)
    position_map = position_in.reshape(slot_count)
    member = (session_map[None, :] == jnp.arange(sessions_dev)[:, None]) & slot_live[None, :]
    queries = query.reshape(sessions_dev, head_dev, HDIM)
    cache_keys = key_cache.reshape(sessions_dev, context, head_dev, HDIM)
    cache_values = value_cache.reshape(sessions_dev, context, head_dev, HDIM)
    own_score = (
        jnp.sum(
            queries.astype(jnp.float32)
            * new_key.reshape(sessions_dev, head_dev, HDIM).astype(jnp.float32),
            axis=-1,
        )
        * inverse_root
    )
    fresh_value = new_value.reshape(sessions_dev, head_dev, HDIM).astype(jnp.float32)
    position_ids = jnp.arange(context)
    target = jnp.where(slot_live, position_map, context)
    key_rows = cache_keys.at[session_map, target].set(restored_keys, mode="drop")
    value_rows = cache_values.at[session_map, target].set(restored_values, mode="drop")
    totals = resident_lengths + jnp.sum(member.astype(jnp.int32), axis=1)
    scores = (
        jnp.einsum("shd,sphd->shp", queries, key_rows, preferred_element_type=jnp.float32)
        * inverse_root
    )
    scores = jnp.where((position_ids[None, :] < totals[:, None])[:, None, :], scores, masked_score)
    highest = jnp.maximum(jnp.max(scores, axis=-1), own_score)
    weights = jnp.exp(scores - highest[:, :, None])
    own_weight = jnp.exp(own_score - highest)
    denominator = jnp.sum(weights, axis=-1) + own_weight
    probability = (weights / denominator[:, :, None]).astype(jnp.bfloat16)
    attended = jnp.einsum(
        "shp,sphd->shd", probability, value_rows, preferred_element_type=jnp.float32
    )
    own_prob = (own_weight / denominator).astype(jnp.bfloat16)
    attended = attended + own_prob.astype(jnp.float32)[:, :, None] * fresh_value
    return attended.astype(jnp.bfloat16).reshape(sessions_dev, head_dev * HDIM)


def solution(mesh):
    placed = (
        P("inst", None, None, "head"),
        P("inst", None),
        P("inst", None, None),
        P("inst", None, None),
        P("inst"),
        P("inst", "head"),
        P("inst", None, "head"),
        P("inst", None, "head"),
        P("inst", "head"),
        P("inst", "head"),
        P("inst", "head"),
    )
    return jax.shard_map(
        local, mesh=mesh, in_specs=placed, out_specs=P("inst", "head"), check_vma=False
    )
```

profile of v0, /device:TPU:1, one launch (start us, length us, event | category | flops | bytes accessed | tf_op | source)
XLA Modules:
  0.0 339.6 jit_solution(13822352009684851430)
XLA Ops:
  6.6 30.2 %all_to_all.40 = bf16[1,32,16,576]{3,2,0,1:T(8,128)(2,1)S(1)} all-to-all(bf16[1,32,16,576]{3,2,0,1:T(8,128)(2,1)} %bitcast.46), channel_id=1, replica_groups=mesh['inst'=32,'head'=16] {'inst'}, dimensions={1} | all-to-all | bytes 1179648 | tf_op jit(solution)/shard_map/all_to_all | solution.py:35
  36.9 1.1 copy.77
  38.0 0.7 all-gather.5.cloned.1.call-update
  38.7 0.7 copy.73
  39.4 8.4 %all-to-all-start.1 = ((s32[1,32,1]{2,0,1:T(1,128)}), s32[1,32,1]{2,0,1:T(1,128)S(1)}, u32[]{:S(2)}, u32[]{:S(2)}) async-start(s32[1,32,1]{2,0,1:T(1,128)} %copy.73), calls=%async_computation.1 | async-start | bytes 32768 | tf_op jit(solution)/shard_map/all_to_all | solution.py:36
  47.9 0.7 copy.72
  48.5 7.9 %all-to-all-done.1 = s32[1,32,1]{2,0,1:T(1,128)S(1)} async-done(((s32[1,32,1]{2,0,1:T(1,128)}), s32[1,32,1]{2,0,1:T(1,128)S(1)}, u32[]{:S(2)}, u32[]{:S(2)}) %all-to-all-start.1) | async-done | bytes 160 | tf_op jit(solution)/shard_map/all_to_all | solution.py:36
  56.4 3.8 %all-to-all-start = ((s32[1,32,16]{2,0,1:T(1,128)}), s32[1,32,16]{2,0,1:T(1,128)S(1)}, u32[]{:S(2)}, u32[]{:S(2)}) async-start(s32[1,32,16]{2,0,1:T(1,128)} %copy.72), calls=%async_computation | async-start | bytes 32768 | tf_op jit(solution)/shard_map/all_to_all | solution.py:37
  60.4 0.7 copy.75
  61.1 0.7 copy.74
  61.9 2.6 copy.79
  64.5 0.7 copy.82
  65.3 2.6 copy.84
  68.8 9.1 %all-to-all-start.2 = ((s32[1,32,16]{2,0,1:T(1,128)}), s32[1,32,16]{2,0,1:T(1,128)S(1)}, u32[]{:S(2)}, u32[]{:S(2)}) async-start(s32[1,32,16]{2,0,1:T(1,128)} %copy.75), calls=%async_computation.2 | async-start | bytes 32768 | tf_op jit(solution)/shard_map/all_to_all | solution.py:38
  78.8 0.7 reduce.10
  79.6 6.8 %all-to-all-done.2 = s32[1,32,16]{2,0,1:T(1,128)S(1)} async-done(((s32[1,32,16]{2,0,1:T(1,128)}), s32[1,32,16]{2,0,1:T(1,128)S(1)}, u32[]{:S(2)}, u32[]{:S(2)}) %all-to-all-start.2) | async-done | bytes 2080 | tf_op jit(solution)/shard_map/all_to_all | solution.py:38
  86.4 0.7 reduce.9
  87.4 15.0 %all-gather.3.cloned.1.call-done = bf16[512,9216]{0,1:T(8,128)(2,1)} async-done(((bf16[512,576]{0,1:T(8,128)(2,1)}), bf16[512,9216]{0,1:T(8,128)(2,1)}) %all-gather.3.cloned.1.call-update) | async-done | bytes 9437200 | tf_op jit(solution)/shard_map/all_gather | solution.py:40
  102.4 135.1 %all-gather.5.cloned.1.call-done = bf16[9216,768]{1,0:T(8,128)(2,1)} async-done(((bf16[288,768]{1,0:T(8,128)(2,1)}), bf16[9216,768]{1,0:T(8,128)(2,1)}) %all-gather.5.cloned.1.call-update) | async-done | bytes 14155792 | tf_op jit(solution)/shard_map/all_gather | solution.py:45
  237.4 14.2 %convolution_convert_fusion = bf16[512,768]{1,0:T(8,128)(2,1)S(1)} fusion(bf16[512,9216]{0,1:T(8,128)(2,1)} %all-gather.3.cloned.1.call-done, bf16[9216,768]{1,0:T(8,128)(2,1)} %all-gather.5.cloned.1.call-done), kind=kOutput, calls=%fused_computation.6 | convolution fusion | flops 7248150528 | bytes 24379392 | tf_op jit(solution)/shard_map/dot_general | solution.py:43
  251.8 1.1 fusion.15
  253.8 55.3 %scatter_fusion = bf16[2,1024,3,128]{3,2,1,0:T(4,128)(2,1)} fusion(bf16[2,1024,3,128]{3,2,1,0:T(4,128)(2,1)} %copy.79, s32[512]{0:T(512)S(1)} %bitcast.41, bf16[512,3,128]{2,1,0:T(4,128)(2,1)S(1)} %copy.80), kind=kCustom, calls=%fused_computation | custom fusion | bytes 1183744 | tf_op jit(solution)/shard_map/scatter | solution.py:69
  309.1 2.1 fusion.2
  311.7 20.1 %scatter_fusion.1 = bf16[2,1024,3,128]{3,2,1,0:T(4,128)(2,1)S(1)} fusion(bf16[2,1024,3,128]{3,2,1,0:T(4,128)(2,1)S(1)} %copy-done, s32[512]{0:T(512)S(1)} %bitcast.42, bf16[512,3,128]{2,1,0:T(4,128)(2,1)S(1)} %copy.85), kind=kCustom, calls=%fused_computation.1 | custom fusion | bytes 1183744 | tf_op jit(solution)/shard_map/scatter | solution.py:70
  (55 shorter events, 5.1 us)
Async XLA Ops:
  6.5 32.2 %copy-start.8 = (s32[1,32]{1,0:T(1,128)S(1)}, s32[1,32]{1,0:T(1,128)}, u32[]{:S(2)}) copy-start(s32[1,32]{1,0:T(1,128)} %param.12) | copy-start | bytes 388
  6.5 41.3 %copy-start.5 = (bf16[2,384]{1,0:T(2,128)(2,1)S(1)}, bf16[2,384]{1,0:T(2,128)(2,1)}, u32[]{:S(2)}) copy-start(bf16[2,384]{1,0:T(2,128)(2,1)} %param.19) | copy-start | bytes 4612
  6.5 41.3 %copy-start.6 = (bf16[2,384]{1,0:T(2,128)(2,1)S(1)}, bf16[2,384]{1,0:T(2,128)(2,1)}, u32[]{:S(2)}) copy-start(bf16[2,384]{1,0:T(2,128)(2,1)} %param.20) | copy-start | bytes 4612
  6.5 41.3 %copy-start.3 = (s32[1,32,16]{1,2,0:T(8,128)S(1)}, s32[1,32,16]{1,2,0:T(8,128)}, u32[]{:S(2)}) copy-start(s32[1,32,16]{1,2,0:T(8,128)} %param.13) | copy-start | bytes 6148
  6.5 53.9 %copy-start.7 = (bf16[2,384]{1,0:T(2,128)(2,1)S(1)}, bf16[2,384]{1,0:T(2,128)(2,1)}, u32[]{:S(2)}) copy-start(bf16[2,384]{1,0:T(2,128)(2,1)} %param.21) | copy-start | bytes 4612
  6.5 53.9 %copy-start.4 = (s32[1,32,16]{1,2,0:T(8,128)S(1)}, s32[1,32,16]{1,2,0:T(8,128)}, u32[]{:S(2)}) copy-start(s32[1,32,16]{1,2,0:T(8,128)} %param.14) | copy-start | bytes 6148
  6.6 54.5 %copy-start.1 = (bf16[2,1024,384]{2,1,0:T(8,128)(2,1)S(1)}, bf16[2,1024,384]{2,1,0:T(8,128)(2,1)}, u32[]{:S(2)}) copy-start(bf16[2,1024,384]{2,1,0:T(8,128)(2,1)} %param.17) | copy-start | bytes 4718596
  6.6 95.8 %all-gather.3.cloned.1.call-start = ((), (), s32[]{:S(2)}) async-start(), calls=%async_computation.4 | async-start | bytes 10027008 | tf_op jit(solution)/shard_map/all_gather | solution.py:40
  37.9 199.5 %all-gather.5.cloned.1.call-start = ((), (), s32[]{:S(2)}) async-start(), calls=%async_computation.5 | async-start | bytes 14598144 | tf_op jit(solution)/shard_map/all_gather | solution.py:45
  39.4 17.0 %all-to-all-start.1 = ((s32[1,32,1]{2,0,1:T(1,128)}), s32[1,32,1]{2,0,1:T(1,128)S(1)}, u32[]{:S(2)}, u32[]{:S(2)}) async-start(s32[1,32,1]{2,0,1:T(1,128)} %copy.73), calls=%async_computation.1 | async-start | bytes 32768 | tf_op jit(solution)/shard_map/all_to_all | solution.py:36
  56.4 12.4 %all-to-all-start = ((s32[1,32,16]{2,0,1:T(1,128)}), s32[1,32,16]{2,0,1:T(1,128)S(1)}, u32[]{:S(2)}, u32[]{:S(2)}) async-start(s32[1,32,16]{2,0,1:T(1,128)} %copy.72), calls=%async_computation | async-start | bytes 32768 | tf_op jit(solution)/shard_map/all_to_all | solution.py:37
  61.9 2.6 copy-start.2
  65.3 22.0 %copy-start.9 = (s32[2]{0:T(128)S(1)}, s32[2]{0:T(128)}, u32[]{:S(2)}) copy-start(s32[2]{0:T(128)} %param.15) | copy-start | bytes 28
  68.8 17.6 %all-to-all-start.2 = ((s32[1,32,16]{2,0,1:T(1,128)}), s32[1,32,16]{2,0,1:T(1,128)S(1)}, u32[]{:S(2)}, u32[]{:S(2)}) async-start(s32[1,32,16]{2,0,1:T(1,128)} %copy.75), calls=%async_computation.2 | async-start | bytes 32768 | tf_op jit(solution)/shard_map/all_to_all | solution.py:38
  253.8 57.9 %copy-start = (bf16[2,1024,3,128]{3,2,1,0:T(4,128)(2,1)S(1)}, bf16[2,1024,3,128]{3,2,1,0:T(4,128)(2,1)}, u32[]{:S(2)}) copy-start(bf16[2,1024,3,128]{3,2,1,0:T(4,128)(2,1)} %copy.84) | copy-start | bytes 4718596
Sparse Core Ops, SparseCore 0:
  38.1 64.2 all-gather.2
  105.5 131.8 all-gather.4
where the time goes:
time: 341 us; the launch traced here: 340 us
  waiting for transfers between devices  166 us (49%)
  local copies, waits for them, and re-layouts  89.1 us (26%)
  blocking collectives  30.2 us (9%)
  starting transfers between devices  21.4 us (6%)
  matrix products  16.6 us (5%)
  between operations  13.6 us (4%)
    all_gather x1, waiting for transfers between devices, local(): lax.all_gather(kv_weight, 'inst', axis=0, tiled=True)  135 us
    scatter x1, local copies, waits for them, and re-layouts, local(): cache_keys.at[session_map, target].set(restored_keys, mode='drop')  55.3 us
    all_to_all x1, blocking collectives, local(): lax.all_to_all(hidden_rows, 'inst', split_axis=1, concat_axis=0, tiled=True)  30.2 us
    scatter x1, local copies, waits for them, and re-layouts, local(): cache_values.at[session_map, target].set(restored_values, mode='drop')  20.1 us
    all_gather x1, waiting for transfers between devices, local(): lax.all_gather(arrived.reshape(slot_count, arrived.shape[3]), 'head', axi...  15 us
    dot_general x1, matrix products, local(): jnp.dot(full_rows, lax.all_gather(kv_weight, 'inst', axis=0, tiled=True),...  14.2 us
    all_to_all x1, starting transfers between devices, local(): lax.all_to_all(row_position, 'inst', split_axis=1, concat_axis=0, tiled=T...  9.1 us
    all_to_all x1, starting transfers between devices, local(): lax.all_to_all(send_counts, 'inst', split_axis=1, concat_axis=0, tiled=True)  8.39 us
  transfers between devices with their start and end apart: 5, of which 5 were waited for; matrix products, arithmetic and copies ran while one was open for 4% of the time, Pallas kernels for 0%

commit v1 on v0

v1 whole, which is shorter than its diff:
```python
import math

import jax
import jax.numpy as jnp
from jax import lax
from jax.experimental import pallas as pl
from jax.experimental.pallas import tpu as pltpu
from jax.sharding import PartitionSpec as P

HDIM = 128
SESS = 2
RES_MAX = 512
ROWS = 8
LOW = -1e30
f32 = jnp.float32
bf16 = jnp.bfloat16
NT = (((1,), (1,)), ((), ()))


def iota(shape, dim):
    return lax.broadcasted_iota(jnp.int32, shape, dim)


def rows_of(shape, heads):
    row = iota(shape, len(shape) - 2) % ROWS
    u = (row >= heads).astype(jnp.int32)
    return u, row - u * heads


def vmem(n):
    return [pl.BlockSpec(memory_space=pltpu.VMEM)] * n


def pack_body(x_ref, q_ref, counts_ref, session_ref, out_ref):
    dests, cap, feats = x_ref.shape
    heads = q_ref.shape[1] // HDIM
    wide = heads * HDIM
    out_ref[:, :, 0:512] = x_ref[:, :, 0:512]
    q = q_ref[...].astype(f32)
    row = iota((cap, wide), 0)
    lane = iota((cap, wide), 1)
    spread = jnp.where(row < 8, q[0:1], q[1:2])
    spread = jnp.where((lane % HDIM) // 16 == row % 8, spread, 0.0)
    src = iota((wide, 64), 0)
    dst = iota((wide, 64), 1)
    fold = ((src // HDIM) * 16 + src % 16 == dst).astype(bf16)
    ext = jnp.dot(spread.astype(bf16), fold, preferred_element_type=f32)
    live = iota((cap, dests), 0) < counts_ref[...]
    code = jnp.where(live, 1 + session_ref[...], 0).astype(f32)
    at = iota((cap, 64), 1) == 48
    for i in range(dests):
        out_ref[i, :, feats : feats + 64] = jnp.where(at, code[:, i : i + 1], ext).astype(bf16)
    out_ref[:, :, 512:feats] = x_ref[:, :, 512:feats]


def qw_body(msg_ref, w_ref, out_ref, wk_ref):
    sources, cap, width = msg_ref.shape
    feats = w_ref.shape[0]
    heads = w_ref.shape[1] // (2 * HDIM)
    wide = heads * HDIM
    odd = lax.axis_index("inst") % 2
    wk_ref[...] = jnp.zeros_like(wk_ref)
    for parity in range(2):

        @pl.when(odd == parity)
        def _():
            for h in range(heads):
                wk_ref[parity * 32 : parity * 32 + feats, h * HDIM : (h + 1) * HDIM] = w_ref[
                    :, 2 * h * HDIM : (2 * h + 1) * HDIM
                ]

    n = sources * cap
    tail = msg_ref[:, :, width - 128 : width].reshape(n, 128)
    src = iota((128, wide), 0) - 64
    dst = iota((128, wide), 1)
    unfold = ((dst // HDIM) * 16 + dst % 16 == src).astype(bf16)
    z = jnp.dot(tail, unfold, preferred_element_type=f32)
    z = jnp.where((iota((n, wide), 1) % HDIM) // 16 == iota((n, wide), 0) % 8, z, 0.0).astype(bf16)
    m = sources * ROWS
    u, h = rows_of((m, n), heads)
    take = (iota((m, n), 0) // ROWS * 2 + u == iota((m, n), 1) // 8).astype(bf16)
    queries = jnp.dot(take, z, preferred_element_type=f32)
    u, h = rows_of((m, wide), heads)
    queries = jnp.where(iota((m, wide), 1) // HDIM == h, queries, 0.0).astype(bf16)
    out = lax.dot_general(queries, wk_ref[...], NT, preferred_element_type=f32)
    out_ref[...] = out.reshape(sources, ROWS, out.shape[1]).astype(bf16)


def cache_body(lengths_ref, q_ref, nk_ref, nv_ref, key_ref, value_ref, out_ref):
    heads = q_ref.shape[1] // HDIM
    wide = heads * HDIM
    span = key_ref.shape[1]
    root = 1.0 / math.sqrt(HDIM)
    u, h = rows_of((ROWS, wide), heads)
    mine = iota((ROWS, wide), 1) // HDIM == h
    q = q_ref[...].astype(f32)
    nk = nk_ref[...].astype(f32)
    nv = nv_ref[...].astype(f32)
    scores = jnp.zeros((ROWS, span), f32)
    own = jnp.zeros((ROWS, 1), f32)
    fresh = jnp.zeros((ROWS, wide), f32)
    for s in range(SESS):
        here = mine & (u == s)
        qs = jnp.where(here, q[s : s + 1], 0.0)
        scores += lax.dot_general(qs.astype(bf16), key_ref[s], NT, preferred_element_type=f32)
        own += jnp.sum(qs * nk[s : s + 1], axis=1, keepdims=True)
        fresh += jnp.where(here, nv[s : s + 1], 0.0)
    scores = scores * root
    us, _ = rows_of((ROWS, span), heads)
    length = jnp.where(us == 0, lengths_ref[0], lengths_ref[1])
    seen = iota((ROWS, span), 1) < length
    scores = jnp.where(seen, scores, LOW)
    top = jnp.max(scores, axis=1, keepdims=True)
    weight = jnp.where(seen, jnp.exp(scores - top), 0.0)
    total = jnp.sum(weight, axis=1, keepdims=True)
    high = weight.astype(bf16).astype(f32)
    both = jnp.concatenate([high, weight - high], axis=0)
    us2 = jnp.concatenate([us, us], axis=0)
    acc = jnp.zeros((2 * ROWS, wide), f32)
    for s in range(SESS):
        part = jnp.where(us2 == s, both, 0.0).astype(bf16)
        acc += jnp.dot(part, value_ref[s], preferred_element_type=f32)
    acc = jnp.where(mine, acc[:ROWS] + acc[ROWS:], 0.0)
    out = jnp.zeros((ROWS, HDIM), f32)
    new = jnp.zeros((ROWS, HDIM), f32)
    for k in range(heads):
        out += acc[:, k * HDIM : (k + 1) * HDIM]
        new += fresh[:, k * HDIM : (k + 1) * HDIM]
    out_ref[0] = out
    out_ref[1] = new
    lane = iota((ROWS, HDIM), 1)
    out_ref[2] = jnp.where(lane == 0, top, jnp.where(lane == 1, total, own * root))


def score_body(qx_ref, msg_ref, out_ref, code_ref):
    sources, cap, width = msg_ref.shape
    n = sources * cap
    blocks = qx_ref.shape[0] // 2
    heads = (ROWS - 2) // SESS
    pad = qx_ref.shape[2]
    q = qx_ref[...].astype(f32).reshape(blocks, 2, ROWS, pad)
    s = jnp.zeros((blocks * ROWS, n), f32)
    for half, at in ((0, 0), (1, width - pad)):
        a = q[:, half].reshape(blocks * ROWS, pad).astype(bf16)
        b = msg_ref[:, :, at : at + pad].reshape(n, pad)
        s += lax.dot_general(a, b, NT, preferred_element_type=f32)
    tail = msg_ref[:, :, width - 128 : width].reshape(n, 128)
    one = (iota((ROWS, 128), 1) == 64 + 48).astype(bf16)
    code = lax.dot_general(one, tail, NT, preferred_element_type=f32)
    code_ref[...] = code
    s = s.reshape(blocks, ROWS, n)
    out_ref[:, 0:heads, :] = jnp.where(code[None, 0:heads] == 2.0, s[:, heads : 2 * heads], s[:, 0:heads])
    out_ref[:, heads : heads + 1, :] = jnp.zeros((blocks, 1, n), f32)


def soft_body(parts_ref, code_ref, cache_ref, out_ref, base_ref):
    heads = (ROWS - 2) // SESS
    n = code_ref.shape[1]
    root = 1.0 / math.sqrt(HDIM)
    s = jnp.sum(parts_ref[...], axis=0) * root
    s = jnp.concatenate([s[0:heads], s[0:heads], s[0:2]], axis=0)
    u, h = rows_of((ROWS, n), heads)
    seen = code_ref[...] == (1 + u).astype(f32)
    s = jnp.where(seen, s, LOW)
    stats = cache_ref[2]
    top_c, total_c, own = stats[:, 0:1], stats[:, 1:2], stats[:, 2:3]
    top = jnp.maximum(jnp.maximum(top_c, own), jnp.max(s, axis=1, keepdims=True))
    weight = jnp.where(seen, jnp.exp(s - top), 0.0)
    scale_c = jnp.exp(top_c - top)
    own_w = jnp.exp(own - top)
    den = jnp.sum(weight, axis=1, keepdims=True) + total_c * scale_c + own_w
    prob = jnp.where(iota((ROWS, n), 0) < SESS * heads, weight / den, 0.0)
    out_ref[...] = jnp.broadcast_to(prob[None], out_ref.shape).astype(bf16)
    own_p = (own_w / den).astype(bf16).astype(f32)
    base_ref[...] = cache_ref[0] * (scale_c / den) + own_p * cache_ref[1]


def mix_body(prob_ref, msg_ref, out_ref):
    sources, cap, width = msg_ref.shape
    n = sources * cap
    blocks = prob_ref.shape[0]
    pad = out_ref.shape[3]
    p = prob_ref[...].astype(f32).reshape(blocks * ROWS, n).astype(bf16)
    for half, at in ((0, 0), (1, width - pad)):
        y = jnp.dot(p, msg_ref[:, :, at : at + pad].reshape(n, pad), preferred_element_type=f32)
        out_ref[:, half] = y.reshape(blocks, ROWS, pad).astype(bf16)


def value_body(y_ref, w_ref, out_ref, wv_ref):
    dests, _, pad = y_ref.shape
    feats = w_ref.shape[0]
    heads = w_ref.shape[1] // (2 * HDIM)
    odd = lax.axis_index("inst") % 2
    wv_ref[...] = jnp.zeros_like(wv_ref)
    for parity in range(2):

        @pl.when(odd == parity)
        def _():
            for h in range(heads):
                wv_ref[parity * 32 : parity * 32 + feats, h * HDIM : (h + 1) * HDIM] = w_ref[
                    :, (2 * h + 1) * HDIM : (2 * h + 2) * HDIM
                ]

    m = dests * ROWS
    y = y_ref[...].astype(f32).reshape(m, pad).astype(bf16)
    r = jnp.dot(y, wv_ref[...], preferred_element_type=f32)
    _, h = rows_of((m, HDIM), heads)
    out = jnp.zeros((m, HDIM), f32)
    for k in range(heads):
        out = jnp.where(h == k, r[:, k * HDIM : (k + 1) * HDIM], out)
    out_ref[...] = out.reshape(dests, ROWS, HDIM)


def last_body(parts_ref, base_ref, out_ref):
    heads = out_ref.shape[1] // HDIM
    t = jnp.sum(parts_ref[...], axis=0) + base_ref[...]
    for h in range(heads):
        both = jnp.concatenate([t[h : h + 1], t[heads + h : heads + h + 1]], axis=0)
        out_ref[:, h * HDIM : (h + 1) * HDIM] = both.astype(bf16)


def local(
    hidden_rows,
    send_counts,
    row_session,
    row_position,
    resident_lengths,
    kv_weight,
    key_cache,
    value_cache,
    query,
    new_key,
    new_value,
):
    _, insts, cap, feats = hidden_rows.shape
    wide = query.shape[1]
    slots = insts * cap
    blocks = lax.axis_size("head")
    pad = 3 * HDIM
    width = feats + 64
    swap = lambda t, axis: lax.all_to_all(t, axis, split_axis=0, concat_axis=0, tiled=True)

    msg = pl.pallas_call(
        pack_body,
        out_shape=jax.ShapeDtypeStruct((insts, cap, width), bf16),
        in_specs=vmem(4),
        out_specs=vmem(1)[0],
    )(hidden_rows[0], query, send_counts, row_session[0].T)
    msg = swap(msg, "inst")

    cache = pl.pallas_call(
        cache_body,
        grid=(1,),
        out_shape=jax.ShapeDtypeStruct((3, ROWS, HDIM), f32),
        in_specs=[pl.BlockSpec(memory_space=pltpu.SMEM)]
        + vmem(3)
        + [pl.BlockSpec((SESS, RES_MAX, wide), lambda i: (0, 0, 0))] * 2,
        out_specs=vmem(1)[0],
    )(resident_lengths, query, new_key, new_value, key_cache, value_cache)

    qw = pl.pallas_call(
        qw_body,
        out_shape=jax.ShapeDtypeStruct((insts, ROWS, pad), bf16),
        in_specs=vmem(2),
        out_specs=vmem(1)[0],
        scratch_shapes=[pltpu.VMEM((pad, wide), bf16)],
    )(msg, kv_weight)
    qx = swap(swap(qw, "inst"), "head")

    part, code = pl.pallas_call(
        score_body,
        out_shape=(
            jax.ShapeDtypeStruct((blocks, 4, slots), f32),
            jax.ShapeDtypeStruct((ROWS, slots), f32),
        ),
        in_specs=vmem(2),
        out_specs=tuple(vmem(2)),
    )(qx, msg)
    part = swap(part, "head")

    prob, base = pl.pallas_call(
        soft_body,
        out_shape=(
            jax.ShapeDtypeStruct((blocks, ROWS, slots), bf16),
            jax.ShapeDtypeStruct((ROWS, HDIM), f32),
        ),
        in_specs=vmem(3),
        out_specs=tuple(vmem(2)),
    )(part, code, cache)
    prob = swap(prob, "head")

    y = pl.pallas_call(
        mix_body,
        out_shape=jax.ShapeDtypeStruct((blocks, 2, ROWS, pad), bf16),
        in_specs=vmem(2),
        out_specs=vmem(1)[0],
    )(prob, msg)
    y = swap(swap(y.reshape(insts, ROWS, pad), "head"), "inst")

    out = pl.pallas_call(
        value_body,
        out_shape=jax.ShapeDtypeStruct((insts, ROWS, HDIM), f32),
        in_specs=vmem(2),
        out_specs=vmem(1)[0],
        scratch_shapes=[pltpu.VMEM((pad, wide), bf16)],
    )(y, kv_weight)
    out = swap(out, "inst")

    return pl.pallas_call(
        last_body,
        out_shape=jax.ShapeDtypeStruct((SESS, wide), bf16),
        in_specs=vmem(2),
        out_specs=vmem(1)[0],
    )(out, base)


def solution(mesh):
    placed = (
        P("inst", None, None, "head"),
        P("inst", None),
        P("inst", None, None),
        P("inst", None, None),
        P("inst"),
        P("inst", "head"),
        P("inst", None, "head"),
        P("inst", None, "head"),
        P("inst", "head"),
        P("inst", "head"),
        P("inst", "head"),
    )
    return jax.shard_map(
        local, mesh=mesh, in_specs=placed, out_specs=P("inst", "head"), check_vma=False
    )
```

time: 341 us -> 152 us (0.45)
  waiting for transfers between devices: 166 us -> 5.83 us
  blocking collectives: 30.2 us -> 123 us
  local copies, waits for them, and re-layouts: 89.1 us -> 0.65 us
  starting transfers between devices: 21.4 us -> 3.41 us
  Pallas kernels: 0 us -> 17.6 us
  matrix products: 16.6 us -> 0 us
  between operations: 13.6 us -> 0.02 us
    all_gather x2 -> x0, waiting for transfers between devices: 150 us -> none  [the longest x1 135 us: local(): lax.all_gather(kv_weight, 'inst', axis=0, tiled=True)]
    all_to_all x1 -> x7, blocking collectives: 30.2 us -> 123 us  [local(): lax.all_to_all(t, axis, split_axis=0, concat_axis=0, tiled=True)]
    scatter x2 -> x0, local copies, waits for them, and re-layouts: 75.4 us -> none  [the longest x1 55.3 us: local(): cache_keys.at[session_map, target].set(restored_keys, mode='drop')]
    all_to_all x3 -> x1, starting transfers between devices: 21.3 us -> 3.41 us  [local(): lax.all_to_all(t, axis, split_axis=0, concat_axis=0, tiled=True)]
    pallas_call x0 -> x8, Pallas kernels: none -> 17.6 us  [the longest x1 2.69 us: local(): pl.pallas_call(cache_body, grid=(1,), out_shape=jax.ShapeDtypeStruct((3,...]
    dot_general x3 -> x0, matrix products: 16.6 us -> none  [the longest x1 14.2 us: local(): jnp.dot(full_rows, lax.all_gather(kv_weight, 'inst', axis=0, tiled=True),...]
    all_to_all x3 -> x1, waiting for transfers between devices: 15 us -> 5.83 us  [local(): lax.all_to_all(t, axis, split_axis=0, concat_axis=0, tiled=True)]
    reshape x8 -> x0, local copies, waits for them, and re-layouts: 6.66 us -> none  [the longest x1 2.63 us: local(): cache_keys = key_cache.reshape(sessions_dev, context, head_dev, HDIM)]
  transfers between devices with their start and end apart: 5 -> 1, of which waited for: 5 -> 1; matrix products, arithmetic and copies ran while one was open for 4% -> 0% of each run, Pallas kernels for 0% -> 2%
where the time goes in v1:
time: 152 us; the launch traced here: 150 us
  blocking collectives  123 us (81%)
  Pallas kernels  17.6 us (12%)
  waiting for transfers between devices  5.83 us (4%)
  starting transfers between devices  3.41 us (2%)
    all_to_all x7, blocking collectives, local(): lax.all_to_all(t, axis, split_axis=0, concat_axis=0, tiled=True)  123 us
    all_to_all x1, waiting for transfers between devices, local(): lax.all_to_all(t, axis, split_axis=0, concat_axis=0, tiled=True)  5.83 us
    all_to_all x1, starting transfers between devices, local(): lax.all_to_all(t, axis, split_axis=0, concat_axis=0, tiled=True)  3.41 us
  transfers between devices with their start and end apart: 1, of which 1 were waited for; matrix products, arithmetic and copies ran while one was open for 0% of the time, Pallas kernels for 2%

profile of v1, /device:TPU:1, one launch (start us, length us, event | category | flops | bytes accessed | tf_op | source)
XLA Modules:
  0.0 150.3 jit_solution(2225840135753323756)
XLA Ops:
  0.0 2.3 %shard_map.100 = bf16[32,16,640]{2,1,0:T(8,128)(2,1)} custom-call(bf16[32,16,576]{2,1,0:T(8,128)(2,1)} %bitcast.6, bf16[2,384]{1,0:T(2,128)(2,1)} %q_ref.3, s32[1,32]{1,0:T(1,128)} %counts_ref.1, s32[16,32]{1,0:T(8,128)} %bitcast.7), custom_call_target="tpu_custom_call" | custom-call | tf_op jit(solution)/shard_map/pallas_call | solution.py:243
  2.3 30.2 %all_to_all.40.msg_ref = bf16[32,16,640]{2,1,0:T(8,128)(2,1)} all-to-all(bf16[32,16,640]{2,1,0:T(8,128)(2,1)} %shard_map.100), channel_id=1, replica_groups=mesh['inst'=32,'head'=16] {'inst'}, dimensions={0} | all-to-all | bytes 1310720 | tf_op jit(solution)/shard_map/all_to_all | solution.py:241
  32.5 2.7 %shard_map.101 = bf16[32,8,384]{2,1,0:T(8,128)(2,1)} custom-call(bf16[32,16,640]{2,1,0:T(8,128)(2,1)} %all_to_all.40.msg_ref, bf16[288,768]{1,0:T(8,128)(2,1)} %w_ref.3), custom_call_target="tpu_custom_call" | custom-call | tf_op jit(solution)/shard_map/pallas_call | solution.py:261
  35.1 17.8 %all_to_all.41 = bf16[32,8,384]{2,1,0:T(8,128)(2,1)S(1)} all-to-all(bf16[32,8,384]{2,1,0:T(8,128)(2,1)} %shard_map.101), channel_id=1, replica_groups=mesh['inst'=32,'head'=16] {'inst'}, dimensions={0} | all-to-all | bytes 393216 | tf_op jit(solution)/shard_map/all_to_all | solution.py:241
  52.9 20.3 %all_to_all.42.qx_ref = bf16[32,8,384]{2,1,0:T(8,128)(2,1)} all-to-all(bf16[32,8,384]{2,1,0:T(8,128)(2,1)S(1)} %all_to_all.41), channel_id=1, replica_groups=mesh['inst'=32,'head'=16] {'head'}, dimensions={0} | all-to-all | bytes 393216 | tf_op jit(solution)/shard_map/all_to_all | solution.py:241
  73.2 2.3 %shard_map.102 = (f32[16,4,512]{2,1,0:T(4,128)}, f32[8,512]{1,0:T(8,128)}) custom-call(bf16[32,8,384]{2,1,0:T(8,128)(2,1)} %all_to_all.42.qx_ref, bf16[32,16,640]{2,1,0:T(8,128)(2,1)} %all_to_all.40.msg_ref), custom_call_target="tpu_custom_call" | custom-call | tf_op jit(solution)/shard_map/pallas_call | solution.py:270
  75.5 3.4 %all-to-all-start.3 = ((f32[16,4,512]{2,1,0:T(4,128)}), f32[16,4,512]{2,1,0:T(4,128)S(1)}, u32[]{:S(2)}, u32[]{:S(2)}) async-start(f32[16,4,512]{2,1,0:T(4,128)} %get-tuple-element.9), calls=%async_computation.3 | async-start | bytes 262144 | tf_op jit(solution)/shard_map/all_to_all | solution.py:241
  78.9 2.7 %shard_map.103.cache_ref = f32[3,8,128]{2,1,0:T(8,128)} custom-call(s32[2]{0:T(128)} %lengths_ref.1, bf16[2,384]{1,0:T(2,128)(2,1)} %q_ref.3, bf16[2,384]{1,0:T(2,128)(2,1)} %nk_ref.1, bf16[2,384]{1,0:T(2,128)(2,1)} %nv_ref.1, bf16[2,1024,384]{2,1,0:T(8,128)(2,1)} %key_ref.1, bf16[2,1024,384]{2,1,0:T(8,128)(2,1)} %value_ref.1), custom_call_target="tpu_custom_call" | custom-call | tf_op jit(solution)/shard_map/pallas_call | solution.py:251
  81.6 5.8 %all-to-all-done.3.parts_ref = f32[16,4,512]{2,1,0:T(4,128)S(1)} async-done(((f32[16,4,512]{2,1,0:T(4,128)}), f32[16,4,512]{2,1,0:T(4,128)S(1)}, u32[]{:S(2)}, u32[]{:S(2)}) %all-to-all-start.3) | async-done | bytes 131104 | tf_op jit(solution)/shard_map/all_to_all | solution.py:241
  87.4 0.0 copy-start
  87.4 0.6 copy-done
  88.0 1.9 %shard_map.104 = (bf16[16,8,512]{2,1,0:T(8,128)(2,1)}, f32[8,128]{1,0:T(8,128)}) custom-call(f32[16,4,512]{2,1,0:T(4,128)} %copy-done, f32[8,512]{1,0:T(8,128)} %get-tuple-element.10.code_ref, f32[3,8,128]{2,1,0:T(8,128)} %shard_map.103.cache_ref), custom_call_target="tpu_custom_call" | custom-call | tf_op jit(solution)/shard_map/pallas_call | solution.py:281
  90.0 13.2 %all_to_all.43.prob_ref = bf16[16,8,512]{2,1,0:T(8,128)(2,1)} all-to-all(bf16[16,8,512]{2,1,0:T(8,128)(2,1)} %get-tuple-element.11), channel_id=1, replica_groups=mesh['inst'=32,'head'=16] {'head'}, dimensions={0} | all-to-all | bytes 262144 | tf_op jit(solution)/shard_map/all_to_all | solution.py:241
  103.2 2.1 %shard_map.105 = bf16[16,2,8,384]{3,2,1,0:T(8,128)(2,1)} custom-call(bf16[16,8,512]{2,1,0:T(8,128)(2,1)} %all_to_all.43.prob_ref, bf16[32,16,640]{2,1,0:T(8,128)(2,1)} %all_to_all.40.msg_ref), custom_call_target="tpu_custom_call" | custom-call | tf_op jit(solution)/shard_map/pallas_call | solution.py:292
  105.3 13.2 %all_to_all.44 = bf16[32,8,384]{2,1,0:T(8,128)(2,1)S(1)} all-to-all(bf16[32,8,384]{2,1,0:T(8,128)(2,1)} %bitcast.5), channel_id=1, replica_groups=mesh['inst'=32,'head'=16] {'head'}, dimensions={0} | all-to-all | bytes 393216 | tf_op jit(solution)/shard_map/all_to_all | solution.py:241
  118.5 13.1 %all_to_all.45.y_ref = bf16[32,8,384]{2,1,0:T(8,128)(2,1)} all-to-all(bf16[32,8,384]{2,1,0:T(8,128)(2,1)S(1)} %all_to_all.44), channel_id=1, replica_groups=mesh['inst'=32,'head'=16] {'inst'}, dimensions={0} | all-to-all | bytes 393216 | tf_op jit(solution)/shard_map/all_to_all | solution.py:241
  131.6 2.1 %shard_map.106 = f32[32,8,128]{2,1,0:T(8,128)} custom-call(bf16[32,8,384]{2,1,0:T(8,128)(2,1)} %all_to_all.45.y_ref, bf16[288,768]{1,0:T(8,128)(2,1)} %w_ref.3), custom_call_target="tpu_custom_call" | custom-call | tf_op jit(solution)/shard_map/pallas_call | solution.py:300
  133.7 15.1 %all_to_all.46.parts_ref = f32[32,8,128]{2,1,0:T(8,128)} all-to-all(f32[32,8,128]{2,1,0:T(8,128)} %shard_map.106), channel_id=1, replica_groups=mesh['inst'=32,'head'=16] {'inst'}, dimensions={0} | all-to-all | bytes 262144 | tf_op jit(solution)/shard_map/all_to_all | solution.py:241
  148.8 1.5 %shard_map.107 = bf16[2,384]{1,0:T(2,128)(2,1)} custom-call(f32[32,8,128]{2,1,0:T(8,128)} %all_to_all.46.parts_ref, f32[8,128]{1,0:T(8,128)} %get-tuple-element.12.base_ref), custom_call_target="tpu_custom_call" | custom-call | tf_op jit(solution)/shard_map/pallas_call | solution.py:309
Async XLA Ops:
  75.5 11.9 %all-to-all-start.3 = ((f32[16,4,512]{2,1,0:T(4,128)}), f32[16,4,512]{2,1,0:T(4,128)S(1)}, u32[]{:S(2)}, u32[]{:S(2)}) async-start(f32[16,4,512]{2,1,0:T(4,128)} %get-tuple-element.9), calls=%async_computation.3 | async-start | bytes 262144 | tf_op jit(solution)/shard_map/all_to_all | solution.py:241
  87.4 0.7 copy-start

commit v2 on v1

--- a/solution.py
+++ b/solution.py
@@ -35,27 +35,31 @@
     dests, cap, feats = x_ref.shape
     heads = q_ref.shape[1] // HDIM
     wide = heads * HDIM
-    out_ref[:, :, 0:512] = x_ref[:, :, 0:512]
+    out_ref[:, :, 0:256] = x_ref[:, :, 0:256]
+    out_ref[:, :, 256:512] = x_ref[:, :, 288:544]
     q = q_ref[...].astype(f32)
     row = iota((cap, wide), 0)
     lane = iota((cap, wide), 1)
     spread = jnp.where(row < 8, q[0:1], q[1:2])
     spread = jnp.where((lane % HDIM) // 16 == row % 8, spread, 0.0)
-    src = iota((wide, 64), 0)
-    dst = iota((wide, 64), 1)
+    src = iota((wide, 128), 0)
+    dst = iota((wide, 128), 1) - 64
     fold = ((src // HDIM) * 16 + src % 16 == dst).astype(bf16)
     ext = jnp.dot(spread.astype(bf16), fold, preferred_element_type=f32)
     live = iota((cap, dests), 0) < counts_ref[...]
     code = jnp.where(live, 1 + session_ref[...], 0).astype(f32)
-    at = iota((cap, 64), 1) == 48
+    lane = iota((cap, 128), 1)
+    none = jnp.zeros((cap, 128 - (feats - 512)), f32)
     for i in range(dests):
-        out_ref[i, :, feats : feats + 64] = jnp.where(at, code[:, i : i + 1], ext).astype(bf16)
-    out_ref[:, :, 512:feats] = x_ref[:, :, 512:feats]
+        low = x_ref[i, :, 256:384].astype(f32)
+        high = jnp.concatenate([x_ref[i, :, 512:feats].astype(f32), none], axis=1)
+        t = jnp.where(lane == 64 + 48, code[:, i : i + 1], ext)
+        t = jnp.where(lane < 32, low, jnp.where(lane < 64, high, t))
+        out_ref[i, :, 512:640] = t.astype(bf16)
 
 
 def qw_body(msg_ref, w_ref, out_ref, wk_ref):
-    sources, cap, width = msg_ref.shape
-    feats = w_ref.shape[0]
+    sources, cap, _ = msg_ref.shape
     heads = w_ref.shape[1] // (2 * HDIM)
     wide = heads * HDIM
     odd = lax.axis_index("inst") % 2
@@ -65,12 +69,14 @@
         @pl.when(odd == parity)
         def _():
             for h in range(heads):
-                wk_ref[parity * 32 : parity * 32 + feats, h * HDIM : (h + 1) * HDIM] = w_ref[
-                    :, 2 * h * HDIM : (2 * h + 1) * HDIM
-                ]
+                at = 256 + parity * 32
+                mine = slice(h * HDIM, (h + 1) * HDIM)
+                keys = slice(2 * h * HDIM, (2 * h + 1) * HDIM)
+                wk_ref[0:256, mine] = w_ref[0:256, keys]
+                wk_ref[at : at + 32, mine] = w_ref[256:288, keys]
 
     n = sources * cap
-    tail = msg_ref[:, :, width - 128 : width].reshape(n, 128)
+    tail = msg_ref[...].reshape(n, 128)
     src = iota((128, wide), 0) - 64
     dst = iota((128, wide), 1)
     unfold = ((dst // HDIM) * 16 + dst % 16 == src).astype(bf16)
@@ -139,11 +145,9 @@
     heads = (ROWS - 2) // SESS
     pad = qx_ref.shape[2]
     q = qx_ref[...].astype(f32).reshape(blocks, 2, ROWS, pad)
-    s = jnp.zeros((blocks * ROWS, n), f32)
-    for half, at in ((0, 0), (1, width - pad)):
-        a = q[:, half].reshape(blocks * ROWS, pad).astype(bf16)
-        b = msg_ref[:, :, at : at + pad].reshape(n, pad)
-        s += lax.dot_general(a, b, NT, preferred_element_type=f32)
+    a = jnp.concatenate([q[:, 0, :, 0:256], q[:, 1, :, 0:256], q[:, 0, :, 256:pad] + q[:, 1, :, 256:pad]], axis=-1)
+    a = a.reshape(blocks * ROWS, width).astype(bf16)
+    s = lax.dot_general(a, msg_ref[...].reshape(n, width), NT, preferred_element_type=f32)
     tail = msg_ref[:, :, width - 128 : width].reshape(n, 128)
     one = (iota((ROWS, 128), 1) == 64 + 48).astype(bf16)
     code = lax.dot_general(one, tail, NT, preferred_element_type=f32)
@@ -179,44 +183,45 @@
     sources, cap, width = msg_ref.shape
     n = sources * cap
     blocks = prob_ref.shape[0]
-    pad = out_ref.shape[3]
     p = prob_ref[...].astype(f32).reshape(blocks * ROWS, n).astype(bf16)
-    for half, at in ((0, 0), (1, width - pad)):
-        y = jnp.dot(p, msg_ref[:, :, at : at + pad].reshape(n, pad), preferred_element_type=f32)
-        out_ref[:, half] = y.reshape(blocks, ROWS, pad).astype(bf16)
-
-
-def value_body(y_ref, w_ref, out_ref, wv_ref):
-    dests, _, pad = y_ref.shape
-    feats = w_ref.shape[0]
-    heads = w_ref.shape[1] // (2 * HDIM)
-    odd = lax.axis_index("inst") % 2
-    wv_ref[...] = jnp.zeros_like(wv_ref)
-    for parity in range(2):
-
-        @pl.when(odd == parity)
-        def _():
-            for h in range(heads):
-                wv_ref[parity * 32 : parity * 32 + feats, h * HDIM : (h + 1) * HDIM] = w_ref[
-                    :, (2 * h + 1) * HDIM : (2 * h + 2) * HDIM
-                ]
-
-    m = dests * ROWS
-    y = y_ref[...].astype(f32).reshape(m, pad).astype(bf16)
-    r = jnp.dot(y, wv_ref[...], preferred_element_type=f32)
-    _, h = rows_of((m, HDIM), heads)
-    out = jnp.zeros((m, HDIM), f32)
+    y = jnp.dot(p, msg_ref[...].reshape(n, width), preferred_element_type=f32)
+    out_ref[...] = y.reshape(blocks, ROWS, width).astype(bf16)
+
+
+def last_body(y_ref, w_ref, base_ref, out_ref, most_ref, rest_ref, most_sem, rest_sem):
+    blocks, _, width = y_ref.shape
+    heads = out_ref.shape[1] // HDIM
+    feats = w_ref.shape[0] // (2 * blocks)
+    copies = []
+    for a in range(2 * blocks):
+        most = pltpu.make_async_copy(
+            w_ref.at[pl.ds(a * feats, 256)], most_ref.at[pl.ds(a * 256, 256)], most_sem.at[a]
+        )
+        rest = pltpu.make_async_copy(
+            w_ref.at[pl.ds(a * feats + 256, 32)],
+            rest_ref.at[pl.ds((a // 2) * 128 + (a % 2) * 32, 32)],
+            rest_sem.at[a],
+        )
+        most.start()
+        rest.start()
+        copies.append((most, rest))
+    for j in range(blocks):
+        rest_ref[j * 128 + 64 : j * 128 + 128] = jnp.zeros((64, rest_ref.shape[1]), bf16)
+    r = jnp.zeros((ROWS, rest_ref.shape[1]), f32)
+    for j in range(blocks):
+        for a in (2 * j, 2 * j + 1):
+            copies[a][0].wait()
+            copies[a][1].wait()
+        y = y_ref[j].astype(f32).astype(bf16)
+        r += jnp.dot(y[:, 0:512], most_ref[j * 512 : (j + 1) * 512], preferred_element_type=f32)
+        r += jnp.dot(y[:, 512:width], rest_ref[j * 128 : (j + 1) * 128], preferred_element_type=f32)
+    _, h = rows_of((ROWS, HDIM), heads)
+    t = base_ref[...]
     for k in range(heads):
-        out = jnp.where(h == k, r[:, k * HDIM : (k + 1) * HDIM], out)
-    out_ref[...] = out.reshape(dests, ROWS, HDIM)
-
-
-def last_body(parts_ref, base_ref, out_ref):
-    heads = out_ref.shape[1] // HDIM
-    t = jnp.sum(parts_ref[...], axis=0) + base_ref[...]
-    for h in range(heads):
-        both = jnp.concatenate([t[h : h + 1], t[heads + h : heads + h + 1]], axis=0)
-        out_ref[:, h * HDIM : (h + 1) * HDIM] = both.astype(bf16)
+        t += jnp.where(h == k, r[:, k * HDIM : (k + 1) * HDIM], 0.0)
+    for k in range(heads):
+        both = jnp.concatenate([t[k : k + 1], t[heads + k : heads + k + 1]], axis=0)
+        out_ref[:, k * HDIM : (k + 1) * HDIM] = both.astype(bf16)
 
 
 def local(
@@ -240,6 +245,9 @@
     width = feats + 64
     swap = lambda t, axis: lax.all_to_all(t, axis, split_axis=0, concat_axis=0, tiled=True)
 
+    values = jnp.concatenate([kv_weight[:, k + HDIM : k + 2 * HDIM] for k in range(0, 2 * wide, 2 * HDIM)], axis=1)
+    values = lax.all_gather(values, "inst", axis=0, tiled=True)
+
     msg = pl.pallas_call(
         pack_body,
         out_shape=jax.ShapeDtypeStruct((insts, cap, width), bf16),
@@ -260,8 +268,9 @@
 
     qw = pl.pallas_call(
         qw_body,
+        grid=(1,),
         out_shape=jax.ShapeDtypeStruct((insts, ROWS, pad), bf16),
-        in_specs=vmem(2),
+        in_specs=[pl.BlockSpec((insts, cap, 128), lambda i: (0, 0, width // 128 - 1)), vmem(1)[0]],
         out_specs=vmem(1)[0],
         scratch_shapes=[pltpu.VMEM((pad, wide), bf16)],
     )(msg, kv_weight)
@@ -291,27 +300,25 @@
 
     y = pl.pallas_call(
         mix_body,
-        out_shape=jax.ShapeDtypeStruct((blocks, 2, ROWS, pad), bf16),
+        out_shape=jax.ShapeDtypeStruct((blocks, ROWS, width), bf16),
         in_specs=vmem(2),
         out_specs=vmem(1)[0],
     )(prob, msg)
-    y = swap(swap(y.reshape(insts, ROWS, pad), "head"), "inst")
-
-    out = pl.pallas_call(
-        value_body,
-        out_shape=jax.ShapeDtypeStruct((insts, ROWS, HDIM), f32),
-        in_specs=vmem(2),
-        out_specs=vmem(1)[0],
-        scratch_shapes=[pltpu.VMEM((pad, wide), bf16)],
-    )(y, kv_weight)
-    out = swap(out, "inst")
+    y = swap(y, "head")
 
     return pl.pallas_call(
         last_body,
         out_shape=jax.ShapeDtypeStruct((SESS, wide), bf16),
-        in_specs=vmem(2),
-        out_specs=vmem(1)[0],
-    )(out, base)
+        in_specs=[vmem(1)[0], pl.BlockSpec(memory_space=pl.ANY), vmem(1)[0]],
+        out_specs=vmem(1)[0],
+        scratch_shapes=[
+            pltpu.VMEM((insts * 256, wide), bf16),
+            pltpu.VMEM((blocks * 128, wide), bf16),
+            pltpu.SemaphoreType.DMA((insts,)),
+            pltpu.SemaphoreType.DMA((insts,)),
+        ],
+        compiler_params=pltpu.CompilerParams(vmem_limit_bytes=56 * 2**20),
+    )(y, values, base)
 
 
 def solution(mesh):

time: 152 us -> 143 us (0.941)
  blocking collectives: 123 us -> 97.5 us
  between operations: 0.02 us -> 13.4 us
  Pallas kernels: 17.6 us -> 19.7 us
    all_to_all x7 -> x5, blocking collectives: 123 us -> 97.5 us  [local(): lax.all_to_all(t, axis, split_axis=0, concat_axis=0, tiled=True)]
    pallas_call x1, Pallas kernels: 1.51 us -> 5.93 us  [local(): pl.pallas_call(last_body, out_shape=jax.ShapeDtypeStruct((SESS, wide), bf...]
    pallas_call x3 -> x2, Pallas kernels: 6.9 us -> 4.63 us  [the longest x1 2.53 us: local(): pl.pallas_call(qw_body, grid=(1,), out_shape=jax.ShapeDtypeStruct((insts,...]
  transfers between devices with their start and end apart: 1 -> 2, of which waited for: 1 -> 1; matrix products, arithmetic and copies ran while one was open for 0% -> 0% of each run, Pallas kernels for 2% -> 10%
where the time goes in v2:
time: 143 us; the launch traced here: 142 us
  blocking collectives  97.5 us (68%)
  Pallas kernels  19.7 us (14%)
  between operations  13.4 us (9%)
  waiting for transfers between devices  5.87 us (4%)
  starting transfers between devices  3.41 us (2%)
  local copies, waits for them, and re-layouts  1.63 us (1%)
    all_to_all x5, blocking collectives, local(): lax.all_to_all(t, axis, split_axis=0, concat_axis=0, tiled=True)  97.5 us
    pallas_call x1, Pallas kernels, local(): pl.pallas_call(last_body, out_shape=jax.ShapeDtypeStruct((SESS, wide), bf...  5.93 us
    all_to_all x1, waiting for transfers between devices, local(): lax.all_to_all(t, axis, split_axis=0, concat_axis=0, tiled=True)  5.86 us
    all_to_all x1, starting transfers between devices, local(): lax.all_to_all(t, axis, split_axis=0, concat_axis=0, tiled=True)  3.41 us
  transfers between devices with their start and end apart: 2, of which 1 were waited for; matrix products, arithmetic and copies ran while one was open for 0% of the time, Pallas kernels for 10%

profile of v2, /device:TPU:1, one launch (start us, length us, event | category | flops | bytes accessed | tf_op | source)
XLA Modules:
  0.0 142.3 jit_solution(1804373311581200948)
XLA Ops:
  6.5 0.0 all-gather.2.cloned.1.call-start
  6.5 1.0 fusion
  7.5 0.7 pad_maximum_fusion
  8.3 0.0 all-gather.2.cloned.1.call-update
  8.3 2.3 %shard_map.100 = bf16[32,16,640]{2,1,0:T(8,128)(2,1)} custom-call(bf16[32,16,576]{2,1,0:T(8,128)(2,1)} %bitcast.4, bf16[2,384]{1,0:T(2,128)(2,1)} %q_ref.3, s32[1,32]{1,0:T(1,128)} %counts_ref.1, s32[16,32]{1,0:T(8,128)} %bitcast.5), custom_call_target="tpu_custom_call" | custom-call | tf_op jit(solution)/shard_map/pallas_call | solution.py:251
  10.5 31.1 %all_to_all.30.msg_ref = bf16[32,16,640]{2,1,0:T(8,128)(2,1)} all-to-all(bf16[32,16,640]{2,1,0:T(8,128)(2,1)} %shard_map.100), channel_id=1, replica_groups=mesh['inst'=32,'head'=16] {'inst'}, dimensions={0} | all-to-all | bytes 1310720 | tf_op jit(solution)/shard_map/all_to_all | solution.py:246
  41.7 2.5 %shard_map.101 = bf16[32,8,384]{2,1,0:T(8,128)(2,1)} custom-call(bf16[32,16,640]{2,1,0:T(8,128)(2,1)} %all_to_all.30.msg_ref, bf16[288,768]{1,0:T(8,128)(2,1)} %w_ref.1), custom_call_target="tpu_custom_call" | custom-call | tf_op jit(solution)/shard_map/pallas_call | solution.py:269
  44.2 19.4 %all_to_all.31 = bf16[32,8,384]{2,1,0:T(8,128)(2,1)S(1)} all-to-all(bf16[32,8,384]{2,1,0:T(8,128)(2,1)} %shard_map.101), channel_id=1, replica_groups=mesh['inst'=32,'head'=16] {'inst'}, dimensions={0} | all-to-all | bytes 393216 | tf_op jit(solution)/shard_map/all_to_all | solution.py:246
  63.6 20.6 %all_to_all.32.qx_ref = bf16[32,8,384]{2,1,0:T(8,128)(2,1)} all-to-all(bf16[32,8,384]{2,1,0:T(8,128)(2,1)S(1)} %all_to_all.31), channel_id=1, replica_groups=mesh['inst'=32,'head'=16] {'head'}, dimensions={0} | all-to-all | bytes 393216 | tf_op jit(solution)/shard_map/all_to_all | solution.py:246
  84.2 2.2 %shard_map.102 = (f32[16,4,512]{2,1,0:T(4,128)}, f32[8,512]{1,0:T(8,128)}) custom-call(bf16[32,8,384]{2,1,0:T(8,128)(2,1)} %all_to_all.32.qx_ref, bf16[32,16,640]{2,1,0:T(8,128)(2,1)} %all_to_all.30.msg_ref), custom_call_target="tpu_custom_call" | custom-call | tf_op jit(solution)/shard_map/pallas_call | solution.py:279
  86.4 3.4 %all-to-all-start.3 = ((f32[16,4,512]{2,1,0:T(4,128)}), f32[16,4,512]{2,1,0:T(4,128)S(1)}, u32[]{:S(2)}, u32[]{:S(2)}) async-start(f32[16,4,512]{2,1,0:T(4,128)} %get-tuple-element.9), calls=%async_computation.3 | async-start | bytes 262144 | tf_op jit(solution)/shard_map/all_to_all | solution.py:246
  89.9 2.7 %shard_map.103.cache_ref = f32[3,8,128]{2,1,0:T(8,128)} custom-call(s32[2]{0:T(128)} %lengths_ref.1, bf16[2,384]{1,0:T(2,128)(2,1)} %q_ref.3, bf16[2,384]{1,0:T(2,128)(2,1)} %nk_ref.1, bf16[2,384]{1,0:T(2,128)(2,1)} %nv_ref.1, bf16[2,1024,384]{2,1,0:T(8,128)(2,1)} %key_ref.1, bf16[2,1024,384]{2,1,0:T(8,128)(2,1)} %value_ref.1), custom_call_target="tpu_custom_call" | custom-call | tf_op jit(solution)/shard_map/pallas_call | solution.py:259
  92.5 5.9 %all-to-all-done.3.parts_ref = f32[16,4,512]{2,1,0:T(4,128)S(1)} async-done(((f32[16,4,512]{2,1,0:T(4,128)}), f32[16,4,512]{2,1,0:T(4,128)S(1)}, u32[]{:S(2)}, u32[]{:S(2)}) %all-to-all-start.3) | async-done | bytes 131104 | tf_op jit(solution)/shard_map/all_to_all | solution.py:246
  98.4 0.0 copy-start
  98.4 0.7 copy-done
  99.1 1.9 %shard_map.104 = (bf16[16,8,512]{2,1,0:T(8,128)(2,1)}, f32[8,128]{1,0:T(8,128)}) custom-call(f32[16,4,512]{2,1,0:T(4,128)} %copy-done, f32[8,512]{1,0:T(8,128)} %get-tuple-element.10.code_ref, f32[3,8,128]{2,1,0:T(8,128)} %shard_map.103.cache_ref), custom_call_target="tpu_custom_call" | custom-call | tf_op jit(solution)/shard_map/pallas_call | solution.py:290
  101.0 13.2 %all_to_all.33.prob_ref = bf16[16,8,512]{2,1,0:T(8,128)(2,1)} all-to-all(bf16[16,8,512]{2,1,0:T(8,128)(2,1)} %get-tuple-element.11), channel_id=1, replica_groups=mesh['inst'=32,'head'=16] {'head'}, dimensions={0} | all-to-all | bytes 262144 | tf_op jit(solution)/shard_map/all_to_all | solution.py:246
  114.2 2.1 %shard_map.105 = bf16[16,8,640]{2,1,0:T(8,128)(2,1)} custom-call(bf16[16,8,512]{2,1,0:T(8,128)(2,1)} %all_to_all.33.prob_ref, bf16[32,16,640]{2,1,0:T(8,128)(2,1)} %all_to_all.30.msg_ref), custom_call_target="tpu_custom_call" | custom-call | tf_op jit(solution)/shard_map/pallas_call | solution.py:301
  116.3 13.2 %all_to_all.34.y_ref = bf16[16,8,640]{2,1,0:T(8,128)(2,1)} all-to-all(bf16[16,8,640]{2,1,0:T(8,128)(2,1)} %shard_map.105), channel_id=1, replica_groups=mesh['inst'=32,'head'=16] {'head'}, dimensions={0} | all-to-all | bytes 327680 | tf_op jit(solution)/shard_map/all_to_all | solution.py:246
  129.5 0.0 all-gather.2.cloned.1.call-done.w_ref
  129.5 5.9 %shard_map.106 = bf16[2,384]{1,0:T(2,128)(2,1)} custom-call(bf16[16,8,640]{2,1,0:T(8,128)(2,1)} %all_to_all.34.y_ref, bf16[9216,384]{1,0:T(8,128)(2,1)} %all-gather.2.cloned.1.call-done.w_ref, f32[8,128]{1,0:T(8,128)} %get-tuple-element.12.base_ref), custom_call_target="tpu_custom_call" | custom-call | tf_op jit(solution)/shard_map/pallas_call | solution.py:309
Async XLA Ops:
  6.5 123.0 %all-gather.2.cloned.1.call-start = ((), (), s32[]{:S(2)}) async-start(), calls=%async_computation.6 | async-start | bytes 7299072 | tf_op jit(solution)/shard_map/all_gather | solution.py:249
  86.4 12.0 %all-to-all-start.3 = ((f32[16,4,512]{2,1,0:T(4,128)}), f32[16,4,512]{2,1,0:T(4,128)S(1)}, u32[]{:S(2)}, u32[]{:S(2)}) async-start(f32[16,4,512]{2,1,0:T(4,128)} %get-tuple-element.9), calls=%async_computation.3 | async-start | bytes 262144 | tf_op jit(solution)/shard_map/all_to_all | solution.py:246
  98.4 0.7 copy-start
Sparse Core Ops, SparseCore 0:
  10.5 105.6 all-gather.1

commit v3 on v2

--- a/solution.py
+++ b/solution.py
@@ -11,6 +11,7 @@
 SESS = 2
 RES_MAX = 512
 ROWS = 8
+GROUP = 4
 LOW = -1e30
 f32 = jnp.float32
 bf16 = jnp.bfloat16
@@ -21,10 +22,15 @@
     return lax.broadcasted_iota(jnp.int32, shape, dim)
 
 
-def rows_of(shape, heads):
+def rows_of(shape):
     row = iota(shape, len(shape) - 2) % ROWS
-    u = (row >= heads).astype(jnp.int32)
-    return u, row - u * heads
+    return row // GROUP, row % GROUP
+
+
+def spare_row(t, heads, part):
+    u, h = rows_of(t.shape)
+    own = jnp.where(u == 0, t[..., heads : heads + 1, :], t[..., GROUP + heads : GROUP + heads + 1, :])
+    return jnp.where(iota(t.shape, t.ndim - 1) // part == h, own, 0.0)
 
 
 def vmem(n):
@@ -58,22 +64,14 @@
         out_ref[i, :, 512:640] = t.astype(bf16)
 
 
-def qw_body(msg_ref, w_ref, out_ref, wk_ref):
+def qw_body(msg_ref, w_ref, out_ref, odd_ref):
     sources, cap, _ = msg_ref.shape
     heads = w_ref.shape[1] // (2 * HDIM)
     wide = heads * HDIM
-    odd = lax.axis_index("inst") % 2
-    wk_ref[...] = jnp.zeros_like(wk_ref)
-    for parity in range(2):
-
-        @pl.when(odd == parity)
-        def _():
-            for h in range(heads):
-                at = 256 + parity * 32
-                mine = slice(h * HDIM, (h + 1) * HDIM)
-                keys = slice(2 * h * HDIM, (2 * h + 1) * HDIM)
-                wk_ref[0:256, mine] = w_ref[0:256, keys]
-                wk_ref[at : at + 32, mine] = w_ref[256:288, keys]
+    odd_ref[...] = jnp.zeros_like(odd_ref)
+    for h in range(heads):
+        odd_ref[h * 32 : h * 32 + 32, h * HDIM : (h + 1) * HDIM] = w_ref[256:288, 2 * h * HDIM : (2 * h + 1) * HDIM]
+    keys = jnp.concatenate([w_ref[0:256, 2 * h * HDIM : (2 * h + 1) * HDIM] for h in range(heads)], axis=1)
 
     n = sources * cap
     tail = msg_ref[...].reshape(n, 128)
@@ -83,13 +81,16 @@
     z = jnp.dot(tail, unfold, preferred_element_type=f32)
     z = jnp.where((iota((n, wide), 1) % HDIM) // 16 == iota((n, wide), 0) % 8, z, 0.0).astype(bf16)
     m = sources * ROWS
-    u, h = rows_of((m, n), heads)
-    take = (iota((m, n), 0) // ROWS * 2 + u == iota((m, n), 1) // 8).astype(bf16)
+    take = (iota((m, n), 0) // GROUP == iota((m, n), 1) // 8).astype(bf16)
     queries = jnp.dot(take, z, preferred_element_type=f32)
-    u, h = rows_of((m, wide), heads)
-    queries = jnp.where(iota((m, wide), 1) // HDIM == h, queries, 0.0).astype(bf16)
-    out = lax.dot_general(queries, wk_ref[...], NT, preferred_element_type=f32)
-    out_ref[...] = out.reshape(sources, ROWS, out.shape[1]).astype(bf16)
+    _, h = rows_of((m, wide))
+    queries = jnp.where((iota((m, wide), 1) // HDIM == h) | (h == heads), queries, 0.0).astype(bf16)
+    even = lax.dot_general(queries, keys, NT, preferred_element_type=f32)
+    odd = lax.dot_general(queries, odd_ref[...], NT, preferred_element_type=f32)
+    _, h = rows_of((m, 128))
+    first = jnp.where(h == heads, odd, even[:, 0:128])
+    out_ref[:, :, 0:128] = first.reshape(sources, ROWS, 128).astype(bf16)
+    out_ref[:, :, 128:256] = even[:, 128:256].reshape(sources, ROWS, 128).astype(bf16)
 
 
 def cache_body(lengths_ref, q_ref, nk_ref, nv_ref, key_ref, value_ref, out_ref):
@@ -97,7 +98,7 @@
     wide = heads * HDIM
     span = key_ref.shape[1]
     root = 1.0 / math.sqrt(HDIM)
-    u, h = rows_of((ROWS, wide), heads)
+    u, h = rows_of((ROWS, wide))
     mine = iota((ROWS, wide), 1) // HDIM == h
     q = q_ref[...].astype(f32)
     nk = nk_ref[...].astype(f32)
@@ -112,7 +113,7 @@
         own += jnp.sum(qs * nk[s : s + 1], axis=1, keepdims=True)
         fresh += jnp.where(here, nv[s : s + 1], 0.0)
     scores = scores * root
-    us, _ = rows_of((ROWS, span), heads)
+    us, _ = rows_of((ROWS, span))
     length = jnp.where(us == 0, lengths_ref[0], lengths_ref[1])
     seen = iota((ROWS, span), 1) < length
     scores = jnp.where(seen, scores, LOW)
@@ -142,28 +143,32 @@
     sources, cap, width = msg_ref.shape
     n = sources * cap
     blocks = qx_ref.shape[0] // 2
-    heads = (ROWS - 2) // SESS
-    pad = qx_ref.shape[2]
-    q = qx_ref[...].astype(f32).reshape(blocks, 2, ROWS, pad)
-    a = jnp.concatenate([q[:, 0, :, 0:256], q[:, 1, :, 0:256], q[:, 0, :, 256:pad] + q[:, 1, :, 256:pad]], axis=-1)
-    a = a.reshape(blocks * ROWS, width).astype(bf16)
+    heads = GROUP - 1
+    q = qx_ref[...].astype(f32).reshape(blocks, 2, ROWS, 256)
+    fold = jnp.concatenate([spare_row(q[:, k, :, 0:128], heads, 32) for k in range(2)], axis=-1)
+    src = iota((256, 128), 0)
+    unfold = ((src // 128) * 32 + src % 32 == iota((256, 128), 1)) & (src % 128 < heads * 32)
+    odd = jnp.dot(
+        fold.reshape(blocks * ROWS, 256).astype(bf16), unfold.astype(bf16), preferred_element_type=f32
+    )
+    even = jnp.concatenate([q[:, 0], q[:, 1]], axis=-1).reshape(blocks * ROWS, 512)
+    a = jnp.concatenate([even.astype(bf16), odd.astype(bf16)], axis=-1)
     s = lax.dot_general(a, msg_ref[...].reshape(n, width), NT, preferred_element_type=f32)
     tail = msg_ref[:, :, width - 128 : width].reshape(n, 128)
     one = (iota((ROWS, 128), 1) == 64 + 48).astype(bf16)
     code = lax.dot_general(one, tail, NT, preferred_element_type=f32)
     code_ref[...] = code
     s = s.reshape(blocks, ROWS, n)
-    out_ref[:, 0:heads, :] = jnp.where(code[None, 0:heads] == 2.0, s[:, heads : 2 * heads], s[:, 0:heads])
-    out_ref[:, heads : heads + 1, :] = jnp.zeros((blocks, 1, n), f32)
+    out_ref[...] = jnp.where(code[None, 0:GROUP] == 2.0, s[:, GROUP:ROWS], s[:, 0:GROUP])
 
 
 def soft_body(parts_ref, code_ref, cache_ref, out_ref, base_ref):
-    heads = (ROWS - 2) // SESS
+    heads = GROUP - 1
     n = code_ref.shape[1]
     root = 1.0 / math.sqrt(HDIM)
     s = jnp.sum(parts_ref[...], axis=0) * root
-    s = jnp.concatenate([s[0:heads], s[0:heads], s[0:2]], axis=0)
-    u, h = rows_of((ROWS, n), heads)
+    s = jnp.concatenate([s, s], axis=0)
+    u, h = rows_of((ROWS, n))
     seen = code_ref[...] == (1 + u).astype(f32)
     s = jnp.where(seen, s, LOW)
     stats = cache_ref[2]
@@ -173,54 +178,76 @@
     scale_c = jnp.exp(top_c - top)
     own_w = jnp.exp(own - top)
     den = jnp.sum(weight, axis=1, keepdims=True) + total_c * scale_c + own_w
-    prob = jnp.where(iota((ROWS, n), 0) < SESS * heads, weight / den, 0.0)
+    prob = jnp.where(h < heads, weight / den, 0.0)
+    prob = prob[0:GROUP] + prob[GROUP:ROWS]
     out_ref[...] = jnp.broadcast_to(prob[None], out_ref.shape).astype(bf16)
     own_p = (own_w / den).astype(bf16).astype(f32)
     base_ref[...] = cache_ref[0] * (scale_c / den) + own_p * cache_ref[1]
 
 
-def mix_body(prob_ref, msg_ref, out_ref):
+def mix_body(prob_ref, code_ref, msg_ref, out_ref):
     sources, cap, width = msg_ref.shape
     n = sources * cap
     blocks = prob_ref.shape[0]
-    p = prob_ref[...].astype(f32).reshape(blocks * ROWS, n).astype(bf16)
+    heads = GROUP - 1
+    p = prob_ref[...].astype(f32)
+    u, _ = rows_of((ROWS, n))
+    p = jnp.where((code_ref[...] == (1 + u).astype(f32))[None], jnp.concatenate([p, p], axis=1), 0.0)
+    p = p.reshape(blocks * ROWS, n).astype(bf16)
     y = jnp.dot(p, msg_ref[...].reshape(n, width), preferred_element_type=f32)
-    out_ref[...] = y.reshape(blocks, ROWS, width).astype(bf16)
+    dst = iota((128, 256), 1)
+    spread = ((iota((128, 256), 0) == dst % 64) & (dst < heads * 64)).astype(bf16)
+    odd = jnp.dot(y[:, 512:640].astype(bf16), spread, preferred_element_type=f32)
+    _, h = rows_of((blocks * ROWS, 256))
+    odd = jnp.where(dst[0:1] // 64 == h, odd, 0.0).reshape(blocks, ROWS, 256)
+    sums = [jnp.sum(odd[:, k : k + GROUP], axis=1, keepdims=True) for k in (0, GROUP)]
+    u, h = rows_of((blocks, ROWS, 256))
+    y = y.reshape(blocks, ROWS, width)
+    first = jnp.where(h == heads, jnp.where(u == 0, sums[0], sums[1]), y[:, :, 0:256])
+    out_ref[:, :, 0:256] = first.astype(bf16)
+    out_ref[:, :, 256:512] = y[:, :, 256:512].astype(bf16)
 
 
 def last_body(y_ref, w_ref, base_ref, out_ref, most_ref, rest_ref, most_sem, rest_sem):
-    blocks, _, width = y_ref.shape
+    blocks = y_ref.shape[0]
+    insts = 2 * blocks
     heads = out_ref.shape[1] // HDIM
-    feats = w_ref.shape[0] // (2 * blocks)
+    wide = heads * HDIM
+    feats = w_ref.shape[0] // insts
     copies = []
-    for a in range(2 * blocks):
+    for a in range(insts):
         most = pltpu.make_async_copy(
             w_ref.at[pl.ds(a * feats, 256)], most_ref.at[pl.ds(a * 256, 256)], most_sem.at[a]
         )
         rest = pltpu.make_async_copy(
-            w_ref.at[pl.ds(a * feats + 256, 32)],
-            rest_ref.at[pl.ds((a // 2) * 128 + (a % 2) * 32, 32)],
-            rest_sem.at[a],
+            w_ref.at[pl.ds(a * feats + 256, 32)], rest_ref.at[pl.ds(a * 32, 32)], rest_sem.at[a]
         )
         most.start()
         rest.start()
         copies.append((most, rest))
-    for j in range(blocks):
-        rest_ref[j * 128 + 64 : j * 128 + 128] = jnp.zeros((64, rest_ref.shape[1]), bf16)
-    r = jnp.zeros((ROWS, rest_ref.shape[1]), f32)
-    for j in range(blocks):
-        for a in (2 * j, 2 * j + 1):
-            copies[a][0].wait()
-            copies[a][1].wait()
-        y = y_ref[j].astype(f32).astype(bf16)
-        r += jnp.dot(y[:, 0:512], most_ref[j * 512 : (j + 1) * 512], preferred_element_type=f32)
-        r += jnp.dot(y[:, 512:width], rest_ref[j * 128 : (j + 1) * 128], preferred_element_type=f32)
-    _, h = rows_of((ROWS, HDIM), heads)
+    y = y_ref[...].astype(f32)
+    fold = spare_row(y[:, :, 0:256], heads, 64).reshape(blocks // 2, 2, ROWS, 256)
+    fold = jnp.concatenate([fold[:, 0], fold[:, 1]], axis=-1).reshape(blocks // 2 * ROWS, 512)
+    src = iota((512, 128), 0)
+    unfold = ((src // 256) * 64 + src % 64 == iota((512, 128), 1)) & (src % 256 < heads * 64)
+    odd = jnp.dot(fold.astype(bf16), unfold.astype(bf16), preferred_element_type=f32)
+    odd = odd.reshape(blocks // 2, ROWS, 128)
+    r = jnp.zeros((ROWS, wide), f32)
+    step = 4
+    for j in range(0, blocks, step):
+        for most, rest in copies[2 * j : 2 * (j + step)]:
+            most.wait()
+            rest.wait()
+        even = jnp.concatenate([y[k] for k in range(j, j + step)], axis=-1).astype(bf16)
+        r += jnp.dot(even, most_ref[j * 512 : (j + step) * 512], preferred_element_type=f32)
+        pair = jnp.concatenate([odd[k] for k in range(j // 2, (j + step) // 2)], axis=-1).astype(bf16)
+        r += jnp.dot(pair, rest_ref[j * 64 : (j + step) * 64], preferred_element_type=f32)
+    _, h = rows_of((ROWS, HDIM))
     t = base_ref[...]
     for k in range(heads):
         t += jnp.where(h == k, r[:, k * HDIM : (k + 1) * HDIM], 0.0)
     for k in range(heads):
-        both = jnp.concatenate([t[k : k + 1], t[heads + k : heads + k + 1]], axis=0)
+        both = jnp.concatenate([t[k : k + 1], t[GROUP + k : GROUP + k + 1]], axis=0)
         out_ref[:, k * HDIM : (k + 1) * HDIM] = both.astype(bf16)
 
 
@@ -241,7 +268,6 @@
     wide = query.shape[1]
     slots = insts * cap
     blocks = lax.axis_size("head")
-    pad = 3 * HDIM
     width = feats + 64
     swap = lambda t, axis: lax.all_to_all(t, axis, split_axis=0, concat_axis=0, tiled=True)
 
@@ -269,17 +295,17 @@
     qw = pl.pallas_call(
         qw_body,
         grid=(1,),
-        out_shape=jax.ShapeDtypeStruct((insts, ROWS, pad), bf16),
+        out_shape=jax.ShapeDtypeStruct((insts, ROWS, 256), bf16),
         in_specs=[pl.BlockSpec((insts, cap, 128), lambda i: (0, 0, width // 128 - 1)), vmem(1)[0]],
         out_specs=vmem(1)[0],
-        scratch_shapes=[pltpu.VMEM((pad, wide), bf16)],
+        scratch_shapes=[pltpu.VMEM((128, wide), bf16)],
     )(msg, kv_weight)
     qx = swap(swap(qw, "inst"), "head")
 
     part, code = pl.pallas_call(
         score_body,
         out_shape=(
-            jax.ShapeDtypeStruct((blocks, 4, slots), f32),
+            jax.ShapeDtypeStruct((blocks, GROUP, slots), f32),
             jax.ShapeDtypeStruct((ROWS, slots), f32),
         ),
         in_specs=vmem(2),
@@ -290,7 +316,7 @@
     prob, base = pl.pallas_call(
         soft_body,
         out_shape=(
-            jax.ShapeDtypeStruct((blocks, ROWS, slots), bf16),
+            jax.ShapeDtypeStruct((blocks, GROUP, slots), bf16),
             jax.ShapeDtypeStruct((ROWS, HDIM), f32),
         ),
         in_specs=vmem(3),
@@ -300,10 +326,10 @@
 
     y = pl.pallas_call(
         mix_body,
-        out_shape=jax.ShapeDtypeStruct((blocks, ROWS, width), bf16),
-        in_specs=vmem(2),
-        out_specs=vmem(1)[0],
-    )(prob, msg)
+        out_shape=jax.ShapeDtypeStruct((blocks, ROWS, 512), bf16),
+        in_specs=vmem(3),
+        out_specs=vmem(1)[0],
+    )(prob, code, msg)
     y = swap(y, "head")
 
     return pl.pallas_call(
@@ -313,7 +339,7 @@
         out_specs=vmem(1)[0],
         scratch_shapes=[
             pltpu.VMEM((insts * 256, wide), bf16),
-            pltpu.VMEM((blocks * 128, wide), bf16),
+            pltpu.VMEM((insts * 32, wide), bf16),
             pltpu.SemaphoreType.DMA((insts,)),
             pltpu.SemaphoreType.DMA((insts,)),
         ],

time: 143 us -> 140 us (0.979)
  blocking collectives: 97.5 us -> 94.9 us
    all_to_all x5, blocking collectives: 97.5 us -> 94.9 us  [local(): lax.all_to_all(t, axis, split_axis=0, concat_axis=0, tiled=True)]
where the time goes in v3:
time: 140 us; the launch traced here: 139 us
  blocking collectives  94.9 us (68%)
  Pallas kernels  19.5 us (14%)
  between operations  13.4 us (10%)
  waiting for transfers between devices  5.75 us (4%)
  starting transfers between devices  3.41 us (2%)
  local copies, waits for them, and re-layouts  1.62 us (1%)
    all_to_all x5, blocking collectives, local(): lax.all_to_all(t, axis, split_axis=0, concat_axis=0, tiled=True)  94.9 us
    all_to_all x1, waiting for transfers between devices, local(): lax.all_to_all(t, axis, split_axis=0, concat_axis=0, tiled=True)  5.73 us
    pallas_call x1, Pallas kernels, local(): pl.pallas_call(last_body, out_shape=jax.ShapeDtypeStruct((SESS, wide), bf...  5.6 us
    all_to_all x1, starting transfers between devices, local(): lax.all_to_all(t, axis, split_axis=0, concat_axis=0, tiled=True)  3.41 us
  transfers between devices with their start and end apart: 2, of which 1 were waited for; matrix products, arithmetic and copies ran while one was open for 0% of the time, Pallas kernels for 10%

profile of v3, /device:TPU:1, one launch (start us, length us, event | category | flops | bytes accessed | tf_op | source)
XLA Modules:
  0.0 139.3 jit_solution(3215477371678777864)
XLA Ops:
  6.5 0.0 all-gather.2.cloned.1.call-start
  6.5 1.0 fusion
  7.5 0.7 pad_maximum_fusion
  8.3 0.0 all-gather.2.cloned.1.call-update
  8.3 2.3 %shard_map.100 = bf16[32,16,640]{2,1,0:T(8,128)(2,1)} custom-call(bf16[32,16,576]{2,1,0:T(8,128)(2,1)} %bitcast.4, bf16[2,384]{1,0:T(2,128)(2,1)} %q_ref.3, s32[1,32]{1,0:T(1,128)} %counts_ref.1, s32[16,32]{1,0:T(8,128)} %bitcast.5), custom_call_target="tpu_custom_call" | custom-call | tf_op jit(solution)/shard_map/pallas_call | solution.py:277
  10.5 31.1 %all_to_all.30.msg_ref = bf16[32,16,640]{2,1,0:T(8,128)(2,1)} all-to-all(bf16[32,16,640]{2,1,0:T(8,128)(2,1)} %shard_map.100), channel_id=1, replica_groups=mesh['inst'=32,'head'=16] {'inst'}, dimensions={0} | all-to-all | bytes 1310720 | tf_op jit(solution)/shard_map/all_to_all | solution.py:272
  41.7 2.4 %shard_map.101 = bf16[32,8,256]{2,1,0:T(8,128)(2,1)} custom-call(bf16[32,16,640]{2,1,0:T(8,128)(2,1)} %all_to_all.30.msg_ref, bf16[288,768]{1,0:T(8,128)(2,1)} %w_ref.1), custom_call_target="tpu_custom_call" | custom-call | tf_op jit(solution)/shard_map/pallas_call | solution.py:295
  44.1 19.4 %all_to_all.31 = bf16[32,8,256]{2,1,0:T(8,128)(2,1)S(1)} all-to-all(bf16[32,8,256]{2,1,0:T(8,128)(2,1)} %shard_map.101), channel_id=1, replica_groups=mesh['inst'=32,'head'=16] {'inst'}, dimensions={0} | all-to-all | bytes 262144 | tf_op jit(solution)/shard_map/all_to_all | solution.py:272
  63.5 19.2 %all_to_all.32.qx_ref = bf16[32,8,256]{2,1,0:T(8,128)(2,1)} all-to-all(bf16[32,8,256]{2,1,0:T(8,128)(2,1)S(1)} %all_to_all.31), channel_id=1, replica_groups=mesh['inst'=32,'head'=16] {'head'}, dimensions={0} | all-to-all | bytes 262144 | tf_op jit(solution)/shard_map/all_to_all | solution.py:272
  82.7 2.2 %shard_map.102 = (f32[16,4,512]{2,1,0:T(4,128)}, f32[8,512]{1,0:T(8,128)}) custom-call(bf16[32,8,256]{2,1,0:T(8,128)(2,1)} %all_to_all.32.qx_ref, bf16[32,16,640]{2,1,0:T(8,128)(2,1)} %all_to_all.30.msg_ref), custom_call_target="tpu_custom_call" | custom-call | tf_op jit(solution)/shard_map/pallas_call | solution.py:305
  84.9 3.4 %all-to-all-start.3 = ((f32[16,4,512]{2,1,0:T(4,128)}), f32[16,4,512]{2,1,0:T(4,128)S(1)}, u32[]{:S(2)}, u32[]{:S(2)}) async-start(f32[16,4,512]{2,1,0:T(4,128)} %get-tuple-element.9), calls=%async_computation.3 | async-start | bytes 262144 | tf_op jit(solution)/shard_map/all_to_all | solution.py:272
  88.3 2.7 %shard_map.103.cache_ref = f32[3,8,128]{2,1,0:T(8,128)} custom-call(s32[2]{0:T(128)} %lengths_ref.1, bf16[2,384]{1,0:T(2,128)(2,1)} %q_ref.3, bf16[2,384]{1,0:T(2,128)(2,1)} %nk_ref.1, bf16[2,384]{1,0:T(2,128)(2,1)} %nv_ref.1, bf16[2,1024,384]{2,1,0:T(8,128)(2,1)} %key_ref.1, bf16[2,1024,384]{2,1,0:T(8,128)(2,1)} %value_ref.1), custom_call_target="tpu_custom_call" | custom-call | tf_op jit(solution)/shard_map/pallas_call | solution.py:285
  91.1 5.7 %all-to-all-done.3.parts_ref = f32[16,4,512]{2,1,0:T(4,128)S(1)} async-done(((f32[16,4,512]{2,1,0:T(4,128)}), f32[16,4,512]{2,1,0:T(4,128)S(1)}, u32[]{:S(2)}, u32[]{:S(2)}) %all-to-all-start.3) | async-done | bytes 131104 | tf_op jit(solution)/shard_map/all_to_all | solution.py:272
  96.8 0.0 copy-start
  96.8 0.6 copy-done
  97.5 1.9 %shard_map.104 = (bf16[16,4,512]{2,1,0:T(4,128)(2,1)}, f32[8,128]{1,0:T(8,128)}) custom-call(f32[16,4,512]{2,1,0:T(4,128)} %copy-done, f32[8,512]{1,0:T(8,128)} %get-tuple-element.10.code_ref, f32[3,8,128]{2,1,0:T(8,128)} %shard_map.103.cache_ref), custom_call_target="tpu_custom_call" | custom-call | tf_op jit(solution)/shard_map/pallas_call | solution.py:316
  99.4 11.8 %all_to_all.33.prob_ref = bf16[16,4,512]{2,1,0:T(4,128)(2,1)} all-to-all(bf16[16,4,512]{2,1,0:T(4,128)(2,1)} %get-tuple-element.11), channel_id=1, replica_groups=mesh['inst'=32,'head'=16] {'head'}, dimensions={0} | all-to-all | bytes 131072 | tf_op jit(solution)/shard_map/all_to_all | solution.py:272
  111.2 2.3 %shard_map.105 = bf16[16,8,512]{2,1,0:T(8,128)(2,1)} custom-call(bf16[16,4,512]{2,1,0:T(4,128)(2,1)} %all_to_all.33.prob_ref, f32[8,512]{1,0:T(8,128)} %get-tuple-element.10.code_ref, bf16[32,16,640]{2,1,0:T(8,128)(2,1)} %all_to_all.30.msg_ref), custom_call_target="tpu_custom_call" | custom-call | tf_op jit(solution)/shard_map/pallas_call | solution.py:327
  113.5 13.4 %all_to_all.34.y_ref = bf16[16,8,512]{2,1,0:T(8,128)(2,1)} all-to-all(bf16[16,8,512]{2,1,0:T(8,128)(2,1)} %shard_map.105), channel_id=1, replica_groups=mesh['inst'=32,'head'=16] {'head'}, dimensions={0} | all-to-all | bytes 262144 | tf_op jit(solution)/shard_map/all_to_all | solution.py:272
  126.8 0.0 all-gather.2.cloned.1.call-done.w_ref
  126.8 5.6 %shard_map.106 = bf16[2,384]{1,0:T(2,128)(2,1)} custom-call(bf16[16,8,512]{2,1,0:T(8,128)(2,1)} %all_to_all.34.y_ref, bf16[9216,384]{1,0:T(8,128)(2,1)} %all-gather.2.cloned.1.call-done.w_ref, f32[8,128]{1,0:T(8,128)} %get-tuple-element.12.base_ref), custom_call_target="tpu_custom_call" | custom-call | tf_op jit(solution)/shard_map/pallas_call | solution.py:335
Async XLA Ops:
  6.5 120.3 %all-gather.2.cloned.1.call-start = ((), (), s32[]{:S(2)}) async-start(), calls=%async_computation.6 | async-start | bytes 7299072 | tf_op jit(solution)/shard_map/all_gather | solution.py:275
  84.9 11.9 %all-to-all-start.3 = ((f32[16,4,512]{2,1,0:T(4,128)}), f32[16,4,512]{2,1,0:T(4,128)S(1)}, u32[]{:S(2)}, u32[]{:S(2)}) async-start(f32[16,4,512]{2,1,0:T(4,128)} %get-tuple-element.9), calls=%async_computation.3 | async-start | bytes 262144 | tf_op jit(solution)/shard_map/all_to_all | solution.py:272
  96.8 0.6 copy-start
Sparse Core Ops, SparseCore 0:
  10.5 105.4 all-gather.1

commit v4 on v3

--- a/solution.py
+++ b/solution.py
@@ -37,12 +37,40 @@
     return [pl.BlockSpec(memory_space=pltpu.VMEM)] * n
 
 
-def pack_body(x_ref, q_ref, counts_ref, session_ref, out_ref):
+MAIN = (((0, 256),), ((224, 64), (32, 64), (96, 128)))
+ODD = (256, 0)
+
+
+def pack_body(x_ref, tail_ref, q_ref, counts_ref, session_ref, w_ref, out_ref, values_ref, new_ref, sem, w_sem):
     dests, cap, feats = x_ref.shape
     heads = q_ref.shape[1] // HDIM
     wide = heads * HDIM
-    out_ref[:, :, 0:256] = x_ref[:, :, 0:256]
-    out_ref[:, :, 256:512] = x_ref[:, :, 288:544]
+    odd = lax.axis_index("inst") % 2
+
+    def moves(parity):
+        out = []
+        at = 0
+        for start, size in MAIN[parity] + ((ODD[parity], 32),):
+            for h in range(heads):
+                out.append(
+                    pltpu.make_async_copy(
+                        w_ref.at[pl.ds(start, size), pl.ds((2 * h + 1) * HDIM, HDIM)],
+                        values_ref.at[pl.ds(at, size), pl.ds(h * HDIM, HDIM)],
+                        w_sem.at[len(out)],
+                    )
+                )
+            at += size
+        return out
+
+    for parity in range(2):
+
+        @pl.when(odd == parity)
+        def _():
+            for move in moves(parity):
+                move.start()
+
+    rows = pltpu.make_async_copy(x_ref.at[:, :, pl.ds(0, 512)], out_ref.at[:, :, pl.ds(0, 512)], sem.at[0])
+    rows.start()
     q = q_ref[...].astype(f32)
     row = iota((cap, wide), 0)
     lane = iota((cap, wide), 1)
@@ -55,26 +83,46 @@
     live = iota((cap, dests), 0) < counts_ref[...]
     code = jnp.where(live, 1 + session_ref[...], 0).astype(f32)
     lane = iota((cap, 128), 1)
-    none = jnp.zeros((cap, 128 - (feats - 512)), f32)
     for i in range(dests):
-        low = x_ref[i, :, 256:384].astype(f32)
-        high = jnp.concatenate([x_ref[i, :, 512:feats].astype(f32), none], axis=1)
         t = jnp.where(lane == 64 + 48, code[:, i : i + 1], ext)
-        t = jnp.where(lane < 32, low, jnp.where(lane < 64, high, t))
-        out_ref[i, :, 512:640] = t.astype(bf16)
-
-
-def qw_body(msg_ref, w_ref, out_ref, odd_ref):
-    sources, cap, _ = msg_ref.shape
+        new_ref[i] = jnp.where(lane < 64, tail_ref[i].astype(f32), t).astype(bf16)
+    tail = pltpu.make_async_copy(new_ref, out_ref.at[:, :, pl.ds(512, 128)], sem.at[1])
+    tail.start()
+    for parity in range(2):
+
+        @pl.when(odd == parity)
+        def _():
+            for move in moves(parity):
+                move.wait()
+
+    rows.wait()
+    tail.wait()
+
+
+def qw_body(msg_ref, w_ref, _, out_ref, main_ref, odd_ref, tail_ref, sem):
+    sources, cap, width = msg_ref.shape
+    fetch = pltpu.make_async_copy(msg_ref.at[:, :, pl.ds(width - 128, 128)], tail_ref, sem)
+    fetch.start()
     heads = w_ref.shape[1] // (2 * HDIM)
     wide = heads * HDIM
+    parity = lax.axis_index("inst") % 2
     odd_ref[...] = jnp.zeros_like(odd_ref)
-    for h in range(heads):
-        odd_ref[h * 32 : h * 32 + 32, h * HDIM : (h + 1) * HDIM] = w_ref[256:288, 2 * h * HDIM : (2 * h + 1) * HDIM]
-    keys = jnp.concatenate([w_ref[0:256, 2 * h * HDIM : (2 * h + 1) * HDIM] for h in range(heads)], axis=1)
+    for p in range(2):
+
+        @pl.when(parity == p)
+        def _():
+            for h in range(heads):
+                mine = slice(h * HDIM, (h + 1) * HDIM)
+                keys = slice(2 * h * HDIM, (2 * h + 1) * HDIM)
+                at = 0
+                for start, size in MAIN[p]:
+                    main_ref[at : at + size, mine] = w_ref[start : start + size, keys]
+                    at += size
+                odd_ref[h * 32 : h * 32 + 32, mine] = w_ref[ODD[p] : ODD[p] + 32, keys]
 
     n = sources * cap
-    tail = msg_ref[...].reshape(n, 128)
+    fetch.wait()
+    tail = tail_ref[...].reshape(n, 128)
     src = iota((128, wide), 0) - 64
     dst = iota((128, wide), 1)
     unfold = ((dst // HDIM) * 16 + dst % 16 == src).astype(bf16)
@@ -85,7 +133,7 @@
     queries = jnp.dot(take, z, preferred_element_type=f32)
     _, h = rows_of((m, wide))
     queries = jnp.where((iota((m, wide), 1) // HDIM == h) | (h == heads), queries, 0.0).astype(bf16)
-    even = lax.dot_general(queries, keys, NT, preferred_element_type=f32)
+    even = lax.dot_general(queries, main_ref[...], NT, preferred_element_type=f32)
     odd = lax.dot_general(queries, odd_ref[...], NT, preferred_element_type=f32)
     _, h = rows_of((m, 128))
     first = jnp.where(h == heads, odd, even[:, 0:128])
@@ -139,8 +187,10 @@
     out_ref[2] = jnp.where(lane == 0, top, jnp.where(lane == 1, total, own * root))
 
 
-def score_body(qx_ref, msg_ref, out_ref, code_ref):
+def score_body(qx_ref, msg_ref, out_ref, code_ref, x_ref, sem):
     sources, cap, width = msg_ref.shape
+    fetch = pltpu.make_async_copy(msg_ref, x_ref, sem)
+    fetch.start()
     n = sources * cap
     blocks = qx_ref.shape[0] // 2
     heads = GROUP - 1
@@ -151,22 +201,29 @@
     odd = jnp.dot(
         fold.reshape(blocks * ROWS, 256).astype(bf16), unfold.astype(bf16), preferred_element_type=f32
     )
-    even = jnp.concatenate([q[:, 0], q[:, 1]], axis=-1).reshape(blocks * ROWS, 512)
-    a = jnp.concatenate([even.astype(bf16), odd.astype(bf16)], axis=-1)
-    s = lax.dot_general(a, msg_ref[...].reshape(n, width), NT, preferred_element_type=f32)
-    tail = msg_ref[:, :, width - 128 : width].reshape(n, 128)
+    even = q[:, 0].reshape(blocks * ROWS, 256)
+    other = q[:, 1].reshape(blocks * ROWS, 256)
+    low = iota(odd.shape, 1) < 64
+    tiles = [even, jnp.where(low, odd, other[:, 0:128]), other[:, 128:256], jnp.where(low, other[:, 0:128], 0.0)]
+    a = jnp.concatenate([t.astype(bf16) for t in tiles], axis=-1)
     one = (iota((ROWS, 128), 1) == 64 + 48).astype(bf16)
+    fetch.wait()
+    s = lax.dot_general(a, x_ref[...].reshape(n, width), NT, preferred_element_type=f32)
+    tail = x_ref[:, :, width - 128 : width].reshape(n, 128)
     code = lax.dot_general(one, tail, NT, preferred_element_type=f32)
     code_ref[...] = code
     s = s.reshape(blocks, ROWS, n)
     out_ref[...] = jnp.where(code[None, 0:GROUP] == 2.0, s[:, GROUP:ROWS], s[:, 0:GROUP])
 
 
-def soft_body(parts_ref, code_ref, cache_ref, out_ref, base_ref):
+def soft_body(parts_ref, code_ref, cache_ref, out_ref, base_ref, here_ref, sem):
+    fetch = pltpu.make_async_copy(parts_ref, here_ref, sem)
+    fetch.start()
     heads = GROUP - 1
     n = code_ref.shape[1]
     root = 1.0 / math.sqrt(HDIM)
-    s = jnp.sum(parts_ref[...], axis=0) * root
+    fetch.wait()
+    s = jnp.sum(here_ref[...], axis=0) * root
     s = jnp.concatenate([s, s], axis=0)
     u, h = rows_of((ROWS, n))
     seen = code_ref[...] == (1 + u).astype(f32)
@@ -185,8 +242,10 @@
     base_ref[...] = cache_ref[0] * (scale_c / den) + own_p * cache_ref[1]
 
 
-def mix_body(prob_ref, code_ref, msg_ref, out_ref):
+def mix_body(prob_ref, code_ref, msg_ref, out_ref, x_ref, sem):
     sources, cap, width = msg_ref.shape
+    fetch = pltpu.make_async_copy(msg_ref, x_ref, sem)
+    fetch.start()
     n = sources * cap
     blocks = prob_ref.shape[0]
     heads = GROUP - 1
@@ -194,10 +253,11 @@
     u, _ = rows_of((ROWS, n))
     p = jnp.where((code_ref[...] == (1 + u).astype(f32))[None], jnp.concatenate([p, p], axis=1), 0.0)
     p = p.reshape(blocks * ROWS, n).astype(bf16)
-    y = jnp.dot(p, msg_ref[...].reshape(n, width), preferred_element_type=f32)
+    fetch.wait()
+    y = jnp.dot(p, x_ref[...].reshape(n, width), preferred_element_type=f32)
     dst = iota((128, 256), 1)
     spread = ((iota((128, 256), 0) == dst % 64) & (dst < heads * 64)).astype(bf16)
-    odd = jnp.dot(y[:, 512:640].astype(bf16), spread, preferred_element_type=f32)
+    odd = jnp.dot(y[:, 256:384].astype(bf16), spread, preferred_element_type=f32)
     _, h = rows_of((blocks * ROWS, 256))
     odd = jnp.where(dst[0:1] // 64 == h, odd, 0.0).reshape(blocks, ROWS, 256)
     sums = [jnp.sum(odd[:, k : k + GROUP], axis=1, keepdims=True) for k in (0, GROUP)]
@@ -205,7 +265,9 @@
     y = y.reshape(blocks, ROWS, width)
     first = jnp.where(h == heads, jnp.where(u == 0, sums[0], sums[1]), y[:, :, 0:256])
     out_ref[:, :, 0:256] = first.astype(bf16)
-    out_ref[:, :, 256:512] = y[:, :, 256:512].astype(bf16)
+    low = iota((blocks, ROWS, 128), 2) < 64
+    out_ref[:, :, 256:384] = jnp.where(low, y[:, :, 512:640], y[:, :, 256:384]).astype(bf16)
+    out_ref[:, :, 384:512] = y[:, :, 384:512].astype(bf16)
 
 
 def last_body(y_ref, w_ref, base_ref, out_ref, most_ref, rest_ref, most_sem, rest_sem):
@@ -232,16 +294,28 @@
     unfold = ((src // 256) * 64 + src % 64 == iota((512, 128), 1)) & (src % 256 < heads * 64)
     odd = jnp.dot(fold.astype(bf16), unfold.astype(bf16), preferred_element_type=f32)
     odd = odd.reshape(blocks // 2, ROWS, 128)
-    r = jnp.zeros((ROWS, wide), f32)
+    extra = jnp.zeros((2 * ROWS, 256), f32)
+
+    def add(left, ref, at, half):
+        first, second = left[:, 0:half], left[:, half : 2 * half]
+        both = jnp.concatenate([first, second], axis=0).astype(bf16)
+        one = jnp.dot(left.astype(bf16), ref[at : at + 2 * half, 0:256], preferred_element_type=f32)
+        pair = jnp.concatenate([ref[at : at + half, 256:384], ref[at + half : at + 2 * half, 256:384]], axis=1)
+        return one, jnp.dot(both, pair, preferred_element_type=f32)
+
+    r = jnp.zeros((ROWS, 256), f32)
     step = 4
     for j in range(0, blocks, step):
         for most, rest in copies[2 * j : 2 * (j + step)]:
             most.wait()
             rest.wait()
-        even = jnp.concatenate([y[k] for k in range(j, j + step)], axis=-1).astype(bf16)
-        r += jnp.dot(even, most_ref[j * 512 : (j + step) * 512], preferred_element_type=f32)
-        pair = jnp.concatenate([odd[k] for k in range(j // 2, (j + step) // 2)], axis=-1).astype(bf16)
-        r += jnp.dot(pair, rest_ref[j * 64 : (j + step) * 64], preferred_element_type=f32)
+        even = jnp.concatenate([y[k] for k in range(j, j + step)], axis=-1)
+        pair = jnp.concatenate([odd[k] for k in range(j // 2, (j + step) // 2)], axis=-1)
+        for left, ref, at in ((even, most_ref, j * 512), (pair, rest_ref, j * 64)):
+            one, two = add(left, ref, at, left.shape[1] // 2)
+            r += one
+            extra += two
+    r = jnp.concatenate([r, extra[0:ROWS, 0:128] + extra[ROWS : 2 * ROWS, 128:256]], axis=1)
     _, h = rows_of((ROWS, HDIM))
     t = base_ref[...]
     for k in range(heads):
@@ -271,15 +345,23 @@
     width = feats + 64
     swap = lambda t, axis: lax.all_to_all(t, axis, split_axis=0, concat_axis=0, tiled=True)
 
-    values = jnp.concatenate([kv_weight[:, k + HDIM : k + 2 * HDIM] for k in range(0, 2 * wide, 2 * HDIM)], axis=1)
+    anywhere = pl.BlockSpec(memory_space=pl.ANY)
+    msg, values = pl.pallas_call(
+        pack_body,
+        grid=(1,),
+        out_shape=(
+            jax.ShapeDtypeStruct((insts, cap, width), bf16),
+            jax.ShapeDtypeStruct((kv_weight.shape[0], wide), bf16),
+        ),
+        in_specs=[anywhere, pl.BlockSpec((insts, cap, 128), lambda i: (0, 0, 4))] + vmem(3) + [anywhere],
+        out_specs=(anywhere, anywhere),
+        scratch_shapes=[
+            pltpu.VMEM((insts, cap, 128), bf16),
+            pltpu.SemaphoreType.DMA((2,)),
+            pltpu.SemaphoreType.DMA((4 * wide // HDIM,)),
+        ],
+    )(hidden_rows[0], hidden_rows[0], query, send_counts, row_session[0].T, kv_weight)
     values = lax.all_gather(values, "inst", axis=0, tiled=True)
-
-    msg = pl.pallas_call(
-        pack_body,
-        out_shape=jax.ShapeDtypeStruct((insts, cap, width), bf16),
-        in_specs=vmem(4),
-        out_specs=vmem(1)[0],
-    )(hidden_rows[0], query, send_counts, row_session[0].T)
     msg = swap(msg, "inst")
 
     cache = pl.pallas_call(
@@ -294,12 +376,16 @@
 
     qw = pl.pallas_call(
         qw_body,
-        grid=(1,),
         out_shape=jax.ShapeDtypeStruct((insts, ROWS, 256), bf16),
-        in_specs=[pl.BlockSpec((insts, cap, 128), lambda i: (0, 0, width // 128 - 1)), vmem(1)[0]],
+        in_specs=[anywhere, vmem(1)[0], anywhere],
         out_specs=vmem(1)[0],
-        scratch_shapes=[pltpu.VMEM((128, wide), bf16)],
-    )(msg, kv_weight)
+        scratch_shapes=[
+            pltpu.VMEM((256, wide), bf16),
+            pltpu.VMEM((128, wide), bf16),
+            pltpu.VMEM((insts, cap, 128), bf16),
+            pltpu.SemaphoreType.DMA,
+        ],
+    )(msg, kv_weight, cache)
     qx = swap(swap(qw, "inst"), "head")
 
     part, code = pl.pallas_call(
@@ -308,8 +394,9 @@
             jax.ShapeDtypeStruct((blocks, GROUP, slots), f32),
             jax.ShapeDtypeStruct((ROWS, slots), f32),
         ),
-        in_specs=vmem(2),
+        in_specs=[vmem(1)[0], anywhere],
         out_specs=tuple(vmem(2)),
+        scratch_shapes=[pltpu.VMEM((insts, cap, width), bf16), pltpu.SemaphoreType.DMA],
     )(qx, msg)
     part = swap(part, "head")
 
@@ -319,16 +406,18 @@
             jax.ShapeDtypeStruct((blocks, GROUP, slots), bf16),
             jax.ShapeDtypeStruct((ROWS, HDIM), f32),
         ),
-        in_specs=vmem(3),
+        in_specs=[anywhere] + vmem(2),
         out_specs=tuple(vmem(2)),
+        scratch_shapes=[pltpu.VMEM((blocks, GROUP, slots), f32), pltpu.SemaphoreType.DMA],
     )(part, code, cache)
     prob = swap(prob, "head")
 
     y = pl.pallas_call(
         mix_body,
         out_shape=jax.ShapeDtypeStruct((blocks, ROWS, 512), bf16),
-        in_specs=vmem(3),
+        in_specs=vmem(2) + [anywhere],
         out_specs=vmem(1)[0],
+        scratch_shapes=[pltpu.VMEM((insts, cap, width), bf16), pltpu.SemaphoreType.DMA],
     )(prob, code, msg)
     y = swap(y, "head")
 

time: 140 us -> 165 us (1.18)
  Pallas kernels: 19.5 us -> 45.2 us
  blocking collectives: 94.9 us -> 76.1 us
  starting transfers between devices: 3.41 us -> 13.8 us
  waiting for transfers between devices: 5.75 us -> 14.5 us
    pallas_call x2, Pallas kernels: 4.72 us -> 28 us  [the longest x1 24.7 us: local(): pl.pallas_call(pack_body, grid=(1,), out_shape=(jax.ShapeDtypeStruct((ins...]
    all_to_all x5, blocking collectives: 94.9 us -> 76.1 us  [local(): lax.all_to_all(t, axis, split_axis=0, concat_axis=0, tiled=True)]
    all_to_all x1, starting transfers between devices: 3.41 us -> 13.7 us  [local(): lax.all_to_all(t, axis, split_axis=0, concat_axis=0, tiled=True)]
    all_to_all x1, waiting for transfers between devices: 5.73 us -> 14.5 us  [local(): lax.all_to_all(t, axis, split_axis=0, concat_axis=0, tiled=True)]
  transfers between devices with their start and end apart: 2 -> 2, of which waited for: 1 -> 1; matrix products, arithmetic and copies ran while one was open for 0% -> 0% of each run, Pallas kernels for 10% -> 9%
where the time goes in v4:
time: 165 us; the launch traced here: 164 us
  blocking collectives  76.1 us (46%)
  Pallas kernels  45.2 us (27%)
  waiting for transfers between devices  14.5 us (9%)
  starting transfers between devices  13.8 us (8%)
  between operations  13.5 us (8%)
    all_to_all x5, blocking collectives, local(): lax.all_to_all(t, axis, split_axis=0, concat_axis=0, tiled=True)  76.1 us
    pallas_call x1, Pallas kernels, local(): pl.pallas_call(pack_body, grid=(1,), out_shape=(jax.ShapeDtypeStruct((ins...  24.7 us
    all_to_all x1, waiting for transfers between devices, local(): lax.all_to_all(t, axis, split_axis=0, concat_axis=0, tiled=True)  14.5 us
    all_to_all x1, starting transfers between devices, local(): lax.all_to_all(t, axis, split_axis=0, concat_axis=0, tiled=True)  13.7 us
    pallas_call x1, Pallas kernels, local(): pl.pallas_call(last_body, out_shape=jax.ShapeDtypeStruct((SESS, wide), bf...  5.76 us
  transfers between devices with their start and end apart: 2, of which 1 were waited for; matrix products, arithmetic and copies ran while one was open for 0% of the time, Pallas kernels for 9%

profile of v4, /device:TPU:1, one launch (start us, length us, event | category | flops | bytes accessed | tf_op | source)
XLA Modules:
  0.0 163.8 jit_solution(5376716352379073596)
XLA Ops:
  6.5 0.0 all-gather.2.cloned.1.call-start
  6.5 24.7 %shard_map.100 = (bf16[32,16,640]{2,1,0:T(8,128)(2,1)}, bf16[288,384]{1,0:T(8,128)(2,1)}) custom-call(bf16[32,16,576]{2,1,0:T(8,128)(2,1)} %bitcast.4, bf16[32,16,576]{2,1,0:T(8,128)(2,1)} %bitcast.5, bf16[2,384]{1,0:T(2,128)(2,1)} %q_ref.3, s32[1,32]{1,0:T(1,128)} %counts_ref.1, s32[16,32]{1,0:T(8,128)} %bitcast.6, bf16[288,768]{1,0:T(8,128)(2,1)} %w_ref.3), custom_call_target="tpu_custom_call" | custom-call | tf_op jit(solution)/shard_map/pallas_call | solution.py:349
  31.3 0.0 all-gather.2.cloned.1.call-update
  31.3 13.7 %all-to-all-start = ((bf16[32,16,640]{2,1,0:T(8,128)(2,1)}), bf16[32,16,640]{2,1,0:T(8,128)(2,1)S(1)}, u32[]{:S(2)}, u32[]{:S(2)}) async-start(bf16[32,16,640]{2,1,0:T(8,128)(2,1)} %get-tuple-element.11), calls=%async_computation | async-start | bytes 1310720 | tf_op jit(solution)/shard_map/all_to_all | solution.py:346
  45.1 2.7 %shard_map.101._.cache_ref = f32[3,8,128]{2,1,0:T(8,128)} custom-call(s32[2]{0:T(128)} %lengths_ref.1, bf16[2,384]{1,0:T(2,128)(2,1)} %q_ref.3, bf16[2,384]{1,0:T(2,128)(2,1)} %nk_ref.1, bf16[2,384]{1,0:T(2,128)(2,1)} %nv_ref.1, bf16[2,1024,384]{2,1,0:T(8,128)(2,1)} %key_ref.1, bf16[2,1024,384]{2,1,0:T(8,128)(2,1)} %value_ref.1), custom_call_target="tpu_custom_call" | custom-call | tf_op jit(solution)/shard_map/pallas_call | solution.py:367
  47.8 14.5 %all-to-all-done.msg_ref = bf16[32,16,640]{2,1,0:T(8,128)(2,1)S(1)} async-done(((bf16[32,16,640]{2,1,0:T(8,128)(2,1)}), bf16[32,16,640]{2,1,0:T(8,128)(2,1)S(1)}, u32[]{:S(2)}, u32[]{:S(2)}) %all-to-all-start) | async-done | bytes 655392 | tf_op jit(solution)/shard_map/all_to_all | solution.py:346
  62.2 0.0 copy-start
  62.2 0.8 copy-done
  63.1 3.3 %shard_map.102 = bf16[32,8,256]{2,1,0:T(8,128)(2,1)} custom-call(bf16[32,16,640]{2,1,0:T(8,128)(2,1)} %copy-done, bf16[288,768]{1,0:T(8,128)(2,1)} %w_ref.3, f32[3,8,128]{2,1,0:T(8,128)} %shard_map.101._.cache_ref), custom_call_target="tpu_custom_call" | custom-call | tf_op jit(solution)/shard_map/pallas_call | solution.py:377
  66.4 19.3 %all_to_all.30 = bf16[32,8,256]{2,1,0:T(8,128)(2,1)S(1)} all-to-all(bf16[32,8,256]{2,1,0:T(8,128)(2,1)} %shard_map.102), channel_id=1, replica_groups=mesh['inst'=32,'head'=16] {'inst'}, dimensions={0} | all-to-all | bytes 262144 | tf_op jit(solution)/shard_map/all_to_all | solution.py:346
  85.6 19.1 %all_to_all.31.qx_ref = bf16[32,8,256]{2,1,0:T(8,128)(2,1)} all-to-all(bf16[32,8,256]{2,1,0:T(8,128)(2,1)S(1)} %all_to_all.30), channel_id=1, replica_groups=mesh['inst'=32,'head'=16] {'head'}, dimensions={0} | all-to-all | bytes 262144 | tf_op jit(solution)/shard_map/all_to_all | solution.py:346
  104.8 3.1 %shard_map.103 = (f32[16,4,512]{2,1,0:T(4,128)}, f32[8,512]{1,0:T(8,128)}) custom-call(bf16[32,8,256]{2,1,0:T(8,128)(2,1)} %all_to_all.31.qx_ref, bf16[32,16,640]{2,1,0:T(8,128)(2,1)} %copy-done), custom_call_target="tpu_custom_call" | custom-call | tf_op jit(solution)/shard_map/pallas_call | solution.py:391
  107.9 12.6 %all_to_all.32.parts_ref = f32[16,4,512]{2,1,0:T(4,128)} all-to-all(f32[16,4,512]{2,1,0:T(4,128)} %get-tuple-element.12), channel_id=1, replica_groups=mesh['inst'=32,'head'=16] {'head'}, dimensions={0} | all-to-all | bytes 262144 | tf_op jit(solution)/shard_map/all_to_all | solution.py:346
  120.4 2.7 %shard_map.104 = (bf16[16,4,512]{2,1,0:T(4,128)(2,1)}, f32[8,128]{1,0:T(8,128)}) custom-call(f32[16,4,512]{2,1,0:T(4,128)} %all_to_all.32.parts_ref, f32[8,512]{1,0:T(8,128)} %get-tuple-element.13.code_ref, f32[3,8,128]{2,1,0:T(8,128)} %shard_map.101._.cache_ref), custom_call_target="tpu_custom_call" | custom-call | tf_op jit(solution)/shard_map/pallas_call | solution.py:403
  123.1 11.8 %all_to_all.33.prob_ref = bf16[16,4,512]{2,1,0:T(4,128)(2,1)} all-to-all(bf16[16,4,512]{2,1,0:T(4,128)(2,1)} %get-tuple-element.14), channel_id=1, replica_groups=mesh['inst'=32,'head'=16] {'head'}, dimensions={0} | all-to-all | bytes 131072 | tf_op jit(solution)/shard_map/all_to_all | solution.py:346
  134.9 3.0 %shard_map.105 = bf16[16,8,512]{2,1,0:T(8,128)(2,1)} custom-call(bf16[16,4,512]{2,1,0:T(4,128)(2,1)} %all_to_all.33.prob_ref, f32[8,512]{1,0:T(8,128)} %get-tuple-element.13.code_ref, bf16[32,16,640]{2,1,0:T(8,128)(2,1)} %copy-done), custom_call_target="tpu_custom_call" | custom-call | tf_op jit(solution)/shard_map/pallas_call | solution.py:415
  137.9 13.3 %all_to_all.34.y_ref = bf16[16,8,512]{2,1,0:T(8,128)(2,1)} all-to-all(bf16[16,8,512]{2,1,0:T(8,128)(2,1)} %shard_map.105), channel_id=1, replica_groups=mesh['inst'=32,'head'=16] {'head'}, dimensions={0} | all-to-all | bytes 262144 | tf_op jit(solution)/shard_map/all_to_all | solution.py:346
  151.2 0.0 all-gather.2.cloned.1.call-done.w_ref
  151.2 5.8 %shard_map.106 = bf16[2,384]{1,0:T(2,128)(2,1)} custom-call(bf16[16,8,512]{2,1,0:T(8,128)(2,1)} %all_to_all.34.y_ref, bf16[9216,384]{1,0:T(8,128)(2,1)} %all-gather.2.cloned.1.call-done.w_ref, f32[8,128]{1,0:T(8,128)} %get-tuple-element.16.base_ref), custom_call_target="tpu_custom_call" | custom-call | tf_op jit(solution)/shard_map/pallas_call | solution.py:424
Async XLA Ops:
  6.5 144.7 %all-gather.2.cloned.1.call-start = ((), (), s32[]{:S(2)}) async-start(), calls=%async_computation.6 | async-start | bytes 7299072 | tf_op jit(solution)/shard_map/all_gather | solution.py:364
  31.3 30.9 %all-to-all-start = ((bf16[32,16,640]{2,1,0:T(8,128)(2,1)}), bf16[32,16,640]{2,1,0:T(8,128)(2,1)S(1)}, u32[]{:S(2)}, u32[]{:S(2)}) async-start(bf16[32,16,640]{2,1,0:T(8,128)(2,1)} %get-tuple-element.11), calls=%async_computation | async-start | bytes 1310720 | tf_op jit(solution)/shard_map/all_to_all | solution.py:346
  62.2 0.8 copy-start
Sparse Core Ops, SparseCore 0:
  31.4 104.9 all-gather.1

commit v5 on v3

--- a/solution.py
+++ b/solution.py
@@ -37,10 +37,12 @@
     return [pl.BlockSpec(memory_space=pltpu.VMEM)] * n
 
 
-def pack_body(x_ref, q_ref, counts_ref, session_ref, out_ref):
+def pack_body(x_ref, q_ref, counts_ref, session_ref, w_ref, out_ref, values_ref):
     dests, cap, feats = x_ref.shape
     heads = q_ref.shape[1] // HDIM
     wide = heads * HDIM
+    for h in range(heads):
+        values_ref[:, h * HDIM : (h + 1) * HDIM] = w_ref[:, (2 * h + 1) * HDIM : (2 * h + 2) * HDIM]
     out_ref[:, :, 0:256] = x_ref[:, :, 0:256]
     out_ref[:, :, 256:512] = x_ref[:, :, 288:544]
     q = q_ref[...].astype(f32)
@@ -208,23 +210,18 @@
     out_ref[:, :, 256:512] = y[:, :, 256:512].astype(bf16)
 
 
-def last_body(y_ref, w_ref, base_ref, out_ref, most_ref, rest_ref, most_sem, rest_sem):
+def last_body(y_ref, w_ref, base_ref, out_ref, here_ref, sem):
     blocks = y_ref.shape[0]
-    insts = 2 * blocks
     heads = out_ref.shape[1] // HDIM
     wide = heads * HDIM
-    feats = w_ref.shape[0] // insts
+    feats = w_ref.shape[0] // (2 * blocks)
+    chunks = sem.shape[0]
+    step = blocks // chunks
     copies = []
-    for a in range(insts):
-        most = pltpu.make_async_copy(
-            w_ref.at[pl.ds(a * feats, 256)], most_ref.at[pl.ds(a * 256, 256)], most_sem.at[a]
-        )
-        rest = pltpu.make_async_copy(
-            w_ref.at[pl.ds(a * feats + 256, 32)], rest_ref.at[pl.ds(a * 32, 32)], rest_sem.at[a]
-        )
-        most.start()
-        rest.start()
-        copies.append((most, rest))
+    for k in range(chunks):
+        rows = pl.ds(k * 2 * step * feats, 2 * step * feats)
+        copies.append(pltpu.make_async_copy(w_ref.at[rows], here_ref.at[rows], sem.at[k]))
+        copies[-1].start()
     y = y_ref[...].astype(f32)
     fold = spare_row(y[:, :, 0:256], heads, 64).reshape(blocks // 2, 2, ROWS, 256)
     fold = jnp.concatenate([fold[:, 0], fold[:, 1]], axis=-1).reshape(blocks // 2 * ROWS, 512)
@@ -233,15 +230,18 @@
     odd = jnp.dot(fold.astype(bf16), unfold.astype(bf16), preferred_element_type=f32)
     odd = odd.reshape(blocks // 2, ROWS, 128)
     r = jnp.zeros((ROWS, wide), f32)
-    step = 4
-    for j in range(0, blocks, step):
-        for most, rest in copies[2 * j : 2 * (j + step)]:
-            most.wait()
-            rest.wait()
-        even = jnp.concatenate([y[k] for k in range(j, j + step)], axis=-1).astype(bf16)
-        r += jnp.dot(even, most_ref[j * 512 : (j + step) * 512], preferred_element_type=f32)
-        pair = jnp.concatenate([odd[k] for k in range(j // 2, (j + step) // 2)], axis=-1).astype(bf16)
-        r += jnp.dot(pair, rest_ref[j * 64 : (j + step) * 64], preferred_element_type=f32)
+    for k in range(chunks):
+        copies[k].wait()
+        blocks_in = range(k * step, (k + 1) * step)
+        left = [y[j] for j in blocks_in] + [odd[j // 2] for j in blocks_in if j % 2 == 0]
+        ins = [a for j in blocks_in for a in (2 * j, 2 * j + 1)]
+        right = [here_ref[a * feats : a * feats + 256] for a in ins]
+        right += [here_ref[a * feats + 256 : (a + 1) * feats] for a in ins]
+        r += jnp.dot(
+            jnp.concatenate(left, axis=-1).astype(bf16),
+            jnp.concatenate(right, axis=0),
+            preferred_element_type=f32,
+        )
     _, h = rows_of((ROWS, HDIM))
     t = base_ref[...]
     for k in range(heads):
@@ -271,15 +271,16 @@
     width = feats + 64
     swap = lambda t, axis: lax.all_to_all(t, axis, split_axis=0, concat_axis=0, tiled=True)
 
-    values = jnp.concatenate([kv_weight[:, k + HDIM : k + 2 * HDIM] for k in range(0, 2 * wide, 2 * HDIM)], axis=1)
+    msg, values = pl.pallas_call(
+        pack_body,
+        out_shape=(
+            jax.ShapeDtypeStruct((insts, cap, width), bf16),
+            jax.ShapeDtypeStruct((kv_weight.shape[0], wide), bf16),
+        ),
+        in_specs=vmem(5),
+        out_specs=tuple(vmem(2)),
+    )(hidden_rows[0], query, send_counts, row_session[0].T, kv_weight)
     values = lax.all_gather(values, "inst", axis=0, tiled=True)
-
-    msg = pl.pallas_call(
-        pack_body,
-        out_shape=jax.ShapeDtypeStruct((insts, cap, width), bf16),
-        in_specs=vmem(4),
-        out_specs=vmem(1)[0],
-    )(hidden_rows[0], query, send_counts, row_session[0].T)
     msg = swap(msg, "inst")
 
     cache = pl.pallas_call(
@@ -337,12 +338,7 @@
         out_shape=jax.ShapeDtypeStruct((SESS, wide), bf16),
         in_specs=[vmem(1)[0], pl.BlockSpec(memory_space=pl.ANY), vmem(1)[0]],
         out_specs=vmem(1)[0],
-        scratch_shapes=[
-            pltpu.VMEM((insts * 256, wide), bf16),
-            pltpu.VMEM((insts * 32, wide), bf16),
-            pltpu.SemaphoreType.DMA((insts,)),
-            pltpu.SemaphoreType.DMA((insts,)),
-        ],
+        scratch_shapes=[pltpu.VMEM(values.shape, bf16), pltpu.SemaphoreType.DMA((8,))],
         compiler_params=pltpu.CompilerParams(vmem_limit_bytes=56 * 2**20),
     )(y, values, base)
 

time: 140 us -> 137 us (0.979)
  transfers between devices with their start and end apart: 2 -> 2, of which waited for: 1 -> 1; matrix products, arithmetic and copies ran while one was open for 0% -> 0% of each run, Pallas kernels for 10% -> 9%
where the time goes in v5:
time: 137 us; the launch traced here: 136 us
  blocking collectives  94.2 us (69%)
  Pallas kernels  19 us (14%)
  between operations  13.4 us (10%)
  waiting for transfers between devices  5.72 us (4%)
  starting transfers between devices  3.41 us (2%)
    all_to_all x5, blocking collectives, local(): lax.all_to_all(t, axis, split_axis=0, concat_axis=0, tiled=True)  94.2 us
    all_to_all x1, waiting for transfers between devices, local(): lax.all_to_all(t, axis, split_axis=0, concat_axis=0, tiled=True)  5.7 us
    pallas_call x1, Pallas kernels, local(): pl.pallas_call(last_body, out_shape=jax.ShapeDtypeStruct((SESS, wide), bf...  4.84 us
    all_to_all x1, starting transfers between devices, local(): lax.all_to_all(t, axis, split_axis=0, concat_axis=0, tiled=True)  3.41 us
    pallas_call x1, Pallas kernels, local(): pl.pallas_call(cache_body, grid=(1,), out_shape=jax.ShapeDtypeStruct((3,...  2.79 us
  transfers between devices with their start and end apart: 2, of which 1 were waited for; matrix products, arithmetic and copies ran while one was open for 0% of the time, Pallas kernels for 9%

profile of v5, /device:TPU:1, one launch (start us, length us, event | category | flops | bytes accessed | tf_op | source)
XLA Modules:
  0.0 136.4 jit_solution(4585783075176472018)
XLA Ops:
  6.5 0.0 all-gather.2.cloned.1.call-start
  6.5 2.5 %shard_map.100 = (bf16[32,16,640]{2,1,0:T(8,128)(2,1)}, bf16[288,384]{1,0:T(8,128)(2,1)}) custom-call(bf16[32,16,576]{2,1,0:T(8,128)(2,1)} %bitcast.4, bf16[2,384]{1,0:T(2,128)(2,1)} %q_ref.3, s32[1,32]{1,0:T(1,128)} %counts_ref.1, s32[16,32]{1,0:T(8,128)} %bitcast.5, bf16[288,768]{1,0:T(8,128)(2,1)} %w_ref.3), custom_call_target="tpu_custom_call" | custom-call | tf_op jit(solution)/shard_map/pallas_call | solution.py:274
  9.0 0.0 all-gather.2.cloned.1.call-update
  9.1 30.2 %all_to_all.30.msg_ref = bf16[32,16,640]{2,1,0:T(8,128)(2,1)} all-to-all(bf16[32,16,640]{2,1,0:T(8,128)(2,1)} %get-tuple-element.11), channel_id=1, replica_groups=mesh['inst'=32,'head'=16] {'inst'}, dimensions={0} | all-to-all | bytes 1310720 | tf_op jit(solution)/shard_map/all_to_all | solution.py:272
  39.3 2.4 %shard_map.101 = bf16[32,8,256]{2,1,0:T(8,128)(2,1)} custom-call(bf16[32,16,640]{2,1,0:T(8,128)(2,1)} %all_to_all.30.msg_ref, bf16[288,768]{1,0:T(8,128)(2,1)} %w_ref.3), custom_call_target="tpu_custom_call" | custom-call | tf_op jit(solution)/shard_map/pallas_call | solution.py:296
  41.7 20.1 %all_to_all.31 = bf16[32,8,256]{2,1,0:T(8,128)(2,1)S(1)} all-to-all(bf16[32,8,256]{2,1,0:T(8,128)(2,1)} %shard_map.101), channel_id=1, replica_groups=mesh['inst'=32,'head'=16] {'inst'}, dimensions={0} | all-to-all | bytes 262144 | tf_op jit(solution)/shard_map/all_to_all | solution.py:272
  61.8 18.8 %all_to_all.32.qx_ref = bf16[32,8,256]{2,1,0:T(8,128)(2,1)} all-to-all(bf16[32,8,256]{2,1,0:T(8,128)(2,1)S(1)} %all_to_all.31), channel_id=1, replica_groups=mesh['inst'=32,'head'=16] {'head'}, dimensions={0} | all-to-all | bytes 262144 | tf_op jit(solution)/shard_map/all_to_all | solution.py:272
  80.6 2.2 %shard_map.102 = (f32[16,4,512]{2,1,0:T(4,128)}, f32[8,512]{1,0:T(8,128)}) custom-call(bf16[32,8,256]{2,1,0:T(8,128)(2,1)} %all_to_all.32.qx_ref, bf16[32,16,640]{2,1,0:T(8,128)(2,1)} %all_to_all.30.msg_ref), custom_call_target="tpu_custom_call" | custom-call | tf_op jit(solution)/shard_map/pallas_call | solution.py:306
  82.8 3.4 %all-to-all-start.3 = ((f32[16,4,512]{2,1,0:T(4,128)}), f32[16,4,512]{2,1,0:T(4,128)S(1)}, u32[]{:S(2)}, u32[]{:S(2)}) async-start(f32[16,4,512]{2,1,0:T(4,128)} %get-tuple-element.12), calls=%async_computation.3 | async-start | bytes 262144 | tf_op jit(solution)/shard_map/all_to_all | solution.py:272
  86.2 2.8 %shard_map.103.cache_ref = f32[3,8,128]{2,1,0:T(8,128)} custom-call(s32[2]{0:T(128)} %lengths_ref.1, bf16[2,384]{1,0:T(2,128)(2,1)} %q_ref.3, bf16[2,384]{1,0:T(2,128)(2,1)} %nk_ref.1, bf16[2,384]{1,0:T(2,128)(2,1)} %nv_ref.1, bf16[2,1024,384]{2,1,0:T(8,128)(2,1)} %key_ref.1, bf16[2,1024,384]{2,1,0:T(8,128)(2,1)} %value_ref.1), custom_call_target="tpu_custom_call" | custom-call | tf_op jit(solution)/shard_map/pallas_call | solution.py:286
  89.0 5.7 %all-to-all-done.3.parts_ref = f32[16,4,512]{2,1,0:T(4,128)S(1)} async-done(((f32[16,4,512]{2,1,0:T(4,128)}), f32[16,4,512]{2,1,0:T(4,128)S(1)}, u32[]{:S(2)}, u32[]{:S(2)}) %all-to-all-start.3) | async-done | bytes 131104 | tf_op jit(solution)/shard_map/all_to_all | solution.py:272
  94.7 0.0 copy-start
  94.7 0.6 copy-done
  95.3 1.9 %shard_map.104 = (bf16[16,4,512]{2,1,0:T(4,128)(2,1)}, f32[8,128]{1,0:T(8,128)}) custom-call(f32[16,4,512]{2,1,0:T(4,128)} %copy-done, f32[8,512]{1,0:T(8,128)} %get-tuple-element.13.code_ref, f32[3,8,128]{2,1,0:T(8,128)} %shard_map.103.cache_ref), custom_call_target="tpu_custom_call" | custom-call | tf_op jit(solution)/shard_map/pallas_call | solution.py:317
  97.3 11.8 %all_to_all.33.prob_ref = bf16[16,4,512]{2,1,0:T(4,128)(2,1)} all-to-all(bf16[16,4,512]{2,1,0:T(4,128)(2,1)} %get-tuple-element.14), channel_id=1, replica_groups=mesh['inst'=32,'head'=16] {'head'}, dimensions={0} | all-to-all | bytes 131072 | tf_op jit(solution)/shard_map/all_to_all | solution.py:272
  109.1 2.3 %shard_map.105 = bf16[16,8,512]{2,1,0:T(8,128)(2,1)} custom-call(bf16[16,4,512]{2,1,0:T(4,128)(2,1)} %all_to_all.33.prob_ref, f32[8,512]{1,0:T(8,128)} %get-tuple-element.13.code_ref, bf16[32,16,640]{2,1,0:T(8,128)(2,1)} %all_to_all.30.msg_ref), custom_call_target="tpu_custom_call" | custom-call | tf_op jit(solution)/shard_map/pallas_call | solution.py:328
  111.3 13.4 %all_to_all.34.y_ref = bf16[16,8,512]{2,1,0:T(8,128)(2,1)} all-to-all(bf16[16,8,512]{2,1,0:T(8,128)(2,1)} %shard_map.105), channel_id=1, replica_groups=mesh['inst'=32,'head'=16] {'head'}, dimensions={0} | all-to-all | bytes 262144 | tf_op jit(solution)/shard_map/all_to_all | solution.py:272
  124.7 0.0 all-gather.2.cloned.1.call-done.w_ref
  124.7 4.8 %shard_map.106 = bf16[2,384]{1,0:T(2,128)(2,1)} custom-call(bf16[16,8,512]{2,1,0:T(8,128)(2,1)} %all_to_all.34.y_ref, bf16[9216,384]{1,0:T(8,128)(2,1)} %all-gather.2.cloned.1.call-done.w_ref, f32[8,128]{1,0:T(8,128)} %get-tuple-element.16.base_ref), custom_call_target="tpu_custom_call" | custom-call | tf_op jit(solution)/shard_map/pallas_call | solution.py:336
Async XLA Ops:
  6.5 118.2 %all-gather.2.cloned.1.call-start = ((), (), s32[]{:S(2)}) async-start(), calls=%async_computation.6 | async-start | bytes 7299072 | tf_op jit(solution)/shard_map/all_gather | solution.py:283
  82.8 11.9 %all-to-all-start.3 = ((f32[16,4,512]{2,1,0:T(4,128)}), f32[16,4,512]{2,1,0:T(4,128)S(1)}, u32[]{:S(2)}, u32[]{:S(2)}) async-start(f32[16,4,512]{2,1,0:T(4,128)} %get-tuple-element.12), calls=%async_computation.3 | async-start | bytes 262144 | tf_op jit(solution)/shard_map/all_to_all | solution.py:272
  94.7 0.6 copy-start
Sparse Core Ops, SparseCore 0:
  10.5 104.4 all-gather.1

commit v6 on v5

--- a/solution.py
+++ b/solution.py
@@ -31,6 +31,10 @@
     u, h = rows_of(t.shape)
     own = jnp.where(u == 0, t[..., heads : heads + 1, :], t[..., GROUP + heads : GROUP + heads + 1, :])
     return jnp.where(iota(t.shape, t.ndim - 1) // part == h, own, 0.0)
+
+
+def near(*arrays):
+    return [pltpu.with_memory_space_constraint(a, pltpu.VMEM) for a in arrays]
 
 
 def vmem(n):
@@ -67,7 +71,7 @@
 
 
 def qw_body(msg_ref, w_ref, out_ref, odd_ref):
-    sources, cap, _ = msg_ref.shape
+    sources, cap, width = msg_ref.shape
     heads = w_ref.shape[1] // (2 * HDIM)
     wide = heads * HDIM
     odd_ref[...] = jnp.zeros_like(odd_ref)
@@ -76,7 +80,7 @@
     keys = jnp.concatenate([w_ref[0:256, 2 * h * HDIM : (2 * h + 1) * HDIM] for h in range(heads)], axis=1)
 
     n = sources * cap
-    tail = msg_ref[...].reshape(n, 128)
+    tail = msg_ref[:, :, width - 128 : width].reshape(n, 128)
     src = iota((128, wide), 0) - 64
     dst = iota((128, wide), 1)
     unfold = ((dst // HDIM) * 16 + dst % 16 == src).astype(bf16)
@@ -274,7 +278,7 @@
     msg, values = pl.pallas_call(
         pack_body,
         out_shape=(
-            jax.ShapeDtypeStruct((insts, cap, width), bf16),
+            pltpu.VMEM((insts, cap, width), bf16),
             jax.ShapeDtypeStruct((kv_weight.shape[0], wide), bf16),
         ),
         in_specs=vmem(5),
@@ -286,7 +290,7 @@
     cache = pl.pallas_call(
         cache_body,
         grid=(1,),
-        out_shape=jax.ShapeDtypeStruct((3, ROWS, HDIM), f32),
+        out_shape=pltpu.VMEM((3, ROWS, HDIM), f32),
         in_specs=[pl.BlockSpec(memory_space=pltpu.SMEM)]
         + vmem(3)
         + [pl.BlockSpec((SESS, RES_MAX, wide), lambda i: (0, 0, 0))] * 2,
@@ -295,42 +299,41 @@
 
     qw = pl.pallas_call(
         qw_body,
-        grid=(1,),
-        out_shape=jax.ShapeDtypeStruct((insts, ROWS, 256), bf16),
-        in_specs=[pl.BlockSpec((insts, cap, 128), lambda i: (0, 0, width // 128 - 1)), vmem(1)[0]],
+        out_shape=pltpu.VMEM((insts, ROWS, 256), bf16),
+        in_specs=vmem(2),
         out_specs=vmem(1)[0],
         scratch_shapes=[pltpu.VMEM((128, wide), bf16)],
-    )(msg, kv_weight)
+    )(*near(msg), kv_weight)
     qx = swap(swap(qw, "inst"), "head")
 
     part, code = pl.pallas_call(
         score_body,
         out_shape=(
-            jax.ShapeDtypeStruct((blocks, GROUP, slots), f32),
-            jax.ShapeDtypeStruct((ROWS, slots), f32),
+            pltpu.VMEM((blocks, GROUP, slots), f32),
+            pltpu.VMEM((ROWS, slots), f32),
         ),
         in_specs=vmem(2),
         out_specs=tuple(vmem(2)),
-    )(qx, msg)
+    )(*near(qx, msg))
     part = swap(part, "head")
 
     prob, base = pl.pallas_call(
         soft_body,
         out_shape=(
-            jax.ShapeDtypeStruct((blocks, GROUP, slots), bf16),
-            jax.ShapeDtypeStruct((ROWS, HDIM), f32),
+            pltpu.VMEM((blocks, GROUP, slots), bf16),
+            pltpu.VMEM((ROWS, HDIM), f32),
         ),
         in_specs=vmem(3),
         out_specs=tuple(vmem(2)),
-    )(part, code, cache)
+    )(*near(part, code, cache))
     prob = swap(prob, "head")
 
     y = pl.pallas_call(
         mix_body,
-        out_shape=jax.ShapeDtypeStruct((blocks, ROWS, 512), bf16),
+        out_shape=pltpu.VMEM((blocks, ROWS, 512), bf16),
         in_specs=vmem(3),
         out_specs=vmem(1)[0],
-    )(prob, code, msg)
+    )(*near(prob, code, msg))
     y = swap(y, "head")
 
     return pl.pallas_call(
@@ -340,7 +343,7 @@
         out_specs=vmem(1)[0],
         scratch_shapes=[pltpu.VMEM(values.shape, bf16), pltpu.SemaphoreType.DMA((8,))],
         compiler_params=pltpu.CompilerParams(vmem_limit_bytes=56 * 2**20),
-    )(y, values, base)
+    )(*near(y), values, *near(base))
 
 
 def solution(mesh):

time: 137 us -> 126 us (0.920)
  Pallas kernels: 19 us -> 11.9 us
  blocking collectives: 94.2 us -> 90.7 us
    pallas_call x6, Pallas kernels: 14.1 us -> 7.89 us  [the longest x1 2.2 us: local(): pl.pallas_call(pack_body, out_shape=(pltpu.VMEM((insts, cap, width), bf16...]
    all_to_all x5, blocking collectives: 94.2 us -> 90.7 us  [local(): lax.all_to_all(t, axis, split_axis=0, concat_axis=0, tiled=True)]
  transfers between devices with their start and end apart: 2 -> 2, of which waited for: 1 -> 1; matrix products, arithmetic and copies ran while one was open for 0% -> 0% of each run, Pallas kernels for 9% -> 5%
where the time goes in v6:
time: 126 us
  blocking collectives  90.7 us (72%)
  between operations  13.4 us (11%)
  Pallas kernels  11.9 us (9%)
  waiting for transfers between devices  6.4 us (5%)
  starting transfers between devices  3.41 us (3%)
    all_to_all x5, blocking collectives, local(): lax.all_to_all(t, axis, split_axis=0, concat_axis=0, tiled=True)  90.7 us
    all_to_all x1, waiting for transfers between devices, local(): lax.all_to_all(t, axis, split_axis=0, concat_axis=0, tiled=True)  6.39 us
    pallas_call x1, Pallas kernels, local(): pl.pallas_call(last_body, out_shape=jax.ShapeDtypeStruct((SESS, wide), bf...  3.98 us
    all_to_all x1, starting transfers between devices, local(): lax.all_to_all(t, axis, split_axis=0, concat_axis=0, tiled=True)  3.41 us
  transfers between devices with their start and end apart: 2, of which 1 were waited for; matrix products, arithmetic and copies ran while one was open for 0% of the time, Pallas kernels for 5%

profile of v6, /device:TPU:1, one launch (start us, length us, event | category | flops | bytes accessed | tf_op | source)
XLA Modules:
  0.0 125.8 jit_solution(12064891829052975010)
XLA Ops:
  6.5 0.0 all-gather.2.cloned.1.call-start
  6.5 2.2 %shard_map.100 = (bf16[32,16,640]{2,1,0:T(8,128)(2,1)S(1)}, bf16[288,384]{1,0:T(8,128)(2,1)}) custom-call(bf16[32,16,576]{2,1,0:T(8,128)(2,1)} %bitcast.4, bf16[2,384]{1,0:T(2,128)(2,1)} %q_ref.3, s32[1,32]{1,0:T(1,128)} %counts_ref.1, s32[16,32]{1,0:T(8,128)} %bitcast.5, bf16[288,768]{1,0:T(8,128)(2,1)} %w_ref.3), custom_call_target="tpu_custom_call" | custom-call | tf_op jit(solution)/shard_map/pallas_call | solution.py:278
  8.7 0.0 all-gather.2.cloned.1.call-update
  8.8 29.9 %all_to_all.30.msg_ref = bf16[32,16,640]{2,1,0:T(8,128)(2,1)S(1)} all-to-all(bf16[32,16,640]{2,1,0:T(8,128)(2,1)S(1)} %get-tuple-element.11), channel_id=1, replica_groups=mesh['inst'=32,'head'=16] {'inst'}, dimensions={0} | all-to-all | bytes 1310720 | tf_op jit(solution)/shard_map/all_to_all | solution.py:276
  38.7 1.7 %shard_map.101 = bf16[32,8,256]{2,1,0:T(8,128)(2,1)S(1)} custom-call(bf16[32,16,640]{2,1,0:T(8,128)(2,1)S(1)} %all_to_all.30.msg_ref, bf16[288,768]{1,0:T(8,128)(2,1)} %w_ref.3), custom_call_target="tpu_custom_call" | custom-call | tf_op jit(solution)/shard_map/pallas_call | solution.py:300
  40.4 19.3 %all_to_all.31 = bf16[32,8,256]{2,1,0:T(8,128)(2,1)S(1)} all-to-all(bf16[32,8,256]{2,1,0:T(8,128)(2,1)S(1)} %shard_map.101), channel_id=1, replica_groups=mesh['inst'=32,'head'=16] {'inst'}, dimensions={0} | all-to-all | bytes 262144 | tf_op jit(solution)/shard_map/all_to_all | solution.py:276
  59.8 19.2 %all_to_all.32.qx_ref = bf16[32,8,256]{2,1,0:T(8,128)(2,1)S(1)} all-to-all(bf16[32,8,256]{2,1,0:T(8,128)(2,1)S(1)} %all_to_all.31), channel_id=1, replica_groups=mesh['inst'=32,'head'=16] {'head'}, dimensions={0} | all-to-all | bytes 262144 | tf_op jit(solution)/shard_map/all_to_all | solution.py:276
  78.9 1.0 shard_map.102
  79.9 3.4 %all-to-all-start.3 = ((f32[16,4,512]{2,1,0:T(4,128)}), f32[16,4,512]{2,1,0:T(4,128)S(1)}, u32[]{:S(2)}, u32[]{:S(2)}) async-start(f32[16,4,512]{2,1,0:T(4,128)} %get-tuple-element.12), calls=%async_computation.3 | async-start | bytes 262144 | tf_op jit(solution)/shard_map/all_to_all | solution.py:276
  83.3 2.1 %shard_map.103.cache_ref = f32[3,8,128]{2,1,0:T(8,128)S(1)} custom-call(s32[2]{0:T(128)} %lengths_ref.1, bf16[2,384]{1,0:T(2,128)(2,1)} %q_ref.3, bf16[2,384]{1,0:T(2,128)(2,1)} %nk_ref.1, bf16[2,384]{1,0:T(2,128)(2,1)} %nv_ref.1, bf16[2,1024,384]{2,1,0:T(8,128)(2,1)} %key_ref.1, bf16[2,1024,384]{2,1,0:T(8,128)(2,1)} %value_ref.1), custom_call_target="tpu_custom_call" | custom-call | tf_op jit(solution)/shard_map/pallas_call | solution.py:290
  85.4 6.4 %all-to-all-done.3.parts_ref = f32[16,4,512]{2,1,0:T(4,128)S(1)} async-done(((f32[16,4,512]{2,1,0:T(4,128)}), f32[16,4,512]{2,1,0:T(4,128)S(1)}, u32[]{:S(2)}, u32[]{:S(2)}) %all-to-all-start.3) | async-done | bytes 131104 | tf_op jit(solution)/shard_map/all_to_all | solution.py:276
  91.8 0.4 shard_map.104
  92.2 10.5 %all_to_all.33.prob_ref = bf16[16,4,512]{2,1,0:T(4,128)(2,1)S(1)} all-to-all(bf16[16,4,512]{2,1,0:T(4,128)(2,1)S(1)} %get-tuple-element.14), channel_id=1, replica_groups=mesh['inst'=32,'head'=16] {'head'}, dimensions={0} | all-to-all | bytes 131072 | tf_op jit(solution)/shard_map/all_to_all | solution.py:276
  102.7 0.5 shard_map.105
  103.2 11.8 %all_to_all.34.y_ref = bf16[16,8,512]{2,1,0:T(8,128)(2,1)S(1)} all-to-all(bf16[16,8,512]{2,1,0:T(8,128)(2,1)S(1)} %shard_map.105), channel_id=1, replica_groups=mesh['inst'=32,'head'=16] {'head'}, dimensions={0} | all-to-all | bytes 262144 | tf_op jit(solution)/shard_map/all_to_all | solution.py:276
  115.0 0.0 all-gather.2.cloned.1.call-done.w_ref
  115.0 4.0 %shard_map.106 = bf16[2,384]{1,0:T(2,128)(2,1)} custom-call(bf16[16,8,512]{2,1,0:T(8,128)(2,1)S(1)} %all_to_all.34.y_ref, bf16[9216,384]{1,0:T(8,128)(2,1)} %all-gather.2.cloned.1.call-done.w_ref, f32[8,128]{1,0:T(8,128)S(1)} %get-tuple-element.16.base_ref), custom_call_target="tpu_custom_call" | custom-call | tf_op jit(solution)/shard_map/pallas_call | solution.py:339
Async XLA Ops:
  6.5 108.5 %all-gather.2.cloned.1.call-start = ((), (), s32[]{:S(2)}) async-start(), calls=%async_computation.6 | async-start | bytes 7299072 | tf_op jit(solution)/shard_map/all_gather | solution.py:287
  79.9 11.9 %all-to-all-start.3 = ((f32[16,4,512]{2,1,0:T(4,128)}), f32[16,4,512]{2,1,0:T(4,128)S(1)}, u32[]{:S(2)}, u32[]{:S(2)}) async-start(f32[16,4,512]{2,1,0:T(4,128)} %get-tuple-element.12), calls=%async_computation.3 | async-start | bytes 262144 | tf_op jit(solution)/shard_map/all_to_all | solution.py:276
Sparse Core Ops, SparseCore 0:
  10.5 104.3 all-gather.1

commit v7 on v6

--- a/solution.py
+++ b/solution.py
@@ -41,12 +41,10 @@
     return [pl.BlockSpec(memory_space=pltpu.VMEM)] * n
 
 
-def pack_body(x_ref, q_ref, counts_ref, session_ref, w_ref, out_ref, values_ref):
+def pack_body(x_ref, q_ref, counts_ref, session_ref, out_ref):
     dests, cap, feats = x_ref.shape
     heads = q_ref.shape[1] // HDIM
     wide = heads * HDIM
-    for h in range(heads):
-        values_ref[:, h * HDIM : (h + 1) * HDIM] = w_ref[:, (2 * h + 1) * HDIM : (2 * h + 2) * HDIM]
     out_ref[:, :, 0:256] = x_ref[:, :, 0:256]
     out_ref[:, :, 256:512] = x_ref[:, :, 288:544]
     q = q_ref[...].astype(f32)
@@ -202,54 +200,43 @@
     p = p.reshape(blocks * ROWS, n).astype(bf16)
     y = jnp.dot(p, msg_ref[...].reshape(n, width), preferred_element_type=f32)
     dst = iota((128, 256), 1)
-    spread = ((iota((128, 256), 0) == dst % 64) & (dst < heads * 64)).astype(bf16)
-    odd = jnp.dot(y[:, 512:640].astype(bf16), spread, preferred_element_type=f32)
+    spread = (iota((128, 256), 0) == dst // 128 * 32 + dst % 32) & (dst % 128 < heads * 32)
+    odd = jnp.dot(y[:, 512:640].astype(bf16), spread.astype(bf16), preferred_element_type=f32)
     _, h = rows_of((blocks * ROWS, 256))
-    odd = jnp.where(dst[0:1] // 64 == h, odd, 0.0).reshape(blocks, ROWS, 256)
+    odd = jnp.where(dst[0:1] % 128 // 32 == h, odd, 0.0).reshape(blocks, ROWS, 256)
     sums = [jnp.sum(odd[:, k : k + GROUP], axis=1, keepdims=True) for k in (0, GROUP)]
     u, h = rows_of((blocks, ROWS, 256))
+    sums = jnp.where(u == 0, sums[0], sums[1])
+    spare = h[:, :, 0:128] == heads
     y = y.reshape(blocks, ROWS, width)
-    first = jnp.where(h == heads, jnp.where(u == 0, sums[0], sums[1]), y[:, :, 0:256])
-    out_ref[:, :, 0:256] = first.astype(bf16)
-    out_ref[:, :, 256:512] = y[:, :, 256:512].astype(bf16)
-
-
-def last_body(y_ref, w_ref, base_ref, out_ref, here_ref, sem):
-    blocks = y_ref.shape[0]
+    halves = []
+    for half in range(2):
+        first = jnp.where(spare, sums[:, :, half * 128 : half * 128 + 128], y[:, :, half * 256 : half * 256 + 128])
+        halves.append(jnp.concatenate([first, y[:, :, half * 256 + 128 : half * 256 + 256]], axis=-1))
+    out_ref[...] = jnp.stack(halves, axis=1).reshape(2 * blocks, ROWS, 256).astype(bf16)
+
+
+def value_body(y_ref, w_ref, out_ref):
+    dests = y_ref.shape[0]
+    heads = w_ref.shape[1] // (2 * HDIM)
+    m = dests * ROWS
+    y = y_ref[...].astype(f32)
+    fold = spare_row(y[:, :, 0:128], heads, 32).reshape(m, 128).astype(bf16)
+    y = y.reshape(m, 256).astype(bf16)
+    columns = [slice((2 * k + 1) * HDIM, (2 * k + 2) * HDIM) for k in range(heads)]
+    odd = [w_ref[256:288, c] for c in columns] + [jnp.zeros((128 - heads * 32, HDIM), bf16)]
+    out = jnp.dot(fold, jnp.concatenate(odd, axis=0), preferred_element_type=f32)
+    even = jnp.concatenate([w_ref[0:256, c] for c in columns], axis=1)
+    even = jnp.dot(y, even, preferred_element_type=f32)
+    _, h = rows_of((m, HDIM))
+    for k in range(heads):
+        out += jnp.where(h == k, even[:, k * HDIM : (k + 1) * HDIM], 0.0)
+    out_ref[...] = out.reshape(dests, ROWS, HDIM)
+
+
+def last_body(parts_ref, base_ref, out_ref):
     heads = out_ref.shape[1] // HDIM
-    wide = heads * HDIM
-    feats = w_ref.shape[0] // (2 * blocks)
-    chunks = sem.shape[0]
-    step = blocks // chunks
-    copies = []
-    for k in range(chunks):
-        rows = pl.ds(k * 2 * step * feats, 2 * step * feats)
-        copies.append(pltpu.make_async_copy(w_ref.at[rows], here_ref.at[rows], sem.at[k]))
-        copies[-1].start()
-    y = y_ref[...].astype(f32)
-    fold = spare_row(y[:, :, 0:256], heads, 64).reshape(blocks // 2, 2, ROWS, 256)
-    fold = jnp.concatenate([fold[:, 0], fold[:, 1]], axis=-1).reshape(blocks // 2 * ROWS, 512)
-    src = iota((512, 128), 0)
-    unfold = ((src // 256) * 64 + src % 64 == iota((512, 128), 1)) & (src % 256 < heads * 64)
-    odd = jnp.dot(fold.astype(bf16), unfold.astype(bf16), preferred_element_type=f32)
-    odd = odd.reshape(blocks // 2, ROWS, 128)
-    r = jnp.zeros((ROWS, wide), f32)
-    for k in range(chunks):
-        copies[k].wait()
-        blocks_in = range(k * step, (k + 1) * step)
-        left = [y[j] for j in blocks_in] + [odd[j // 2] for j in blocks_in if j % 2 == 0]
-        ins = [a for j in blocks_in for a in (2 * j, 2 * j + 1)]
-        right = [here_ref[a * feats : a * feats + 256] for a in ins]
-        right += [here_ref[a * feats + 256 : (a + 1) * feats] for a in ins]
-        r += jnp.dot(
-            jnp.concatenate(left, axis=-1).astype(bf16),
-            jnp.concatenate(right, axis=0),
-            preferred_element_type=f32,
-        )
-    _, h = rows_of((ROWS, HDIM))
-    t = base_ref[...]
-    for k in range(heads):
-        t += jnp.where(h == k, r[:, k * HDIM : (k + 1) * HDIM], 0.0)
+    t = jnp.sum(parts_ref[...], axis=0) + base_ref[...]
     for k in range(heads):
         both = jnp.concatenate([t[k : k + 1], t[GROUP + k : GROUP + k + 1]], axis=0)
         out_ref[:, k * HDIM : (k + 1) * HDIM] = both.astype(bf16)
@@ -275,16 +262,14 @@
     width = feats + 64
     swap = lambda t, axis: lax.all_to_all(t, axis, split_axis=0, concat_axis=0, tiled=True)
 
-    msg, values = pl.pallas_call(
+    (weight,) = near(kv_weight)
+
+    msg = pl.pallas_call(
         pack_body,
-        out_shape=(
-            pltpu.VMEM((insts, cap, width), bf16),
-            jax.ShapeDtypeStruct((kv_weight.shape[0], wide), bf16),
-        ),
-        in_specs=vmem(5),
-        out_specs=tuple(vmem(2)),
-    )(hidden_rows[0], query, send_counts, row_session[0].T, kv_weight)
-    values = lax.all_gather(values, "inst", axis=0, tiled=True)
+        out_shape=pltpu.VMEM((insts, cap, width), bf16),
+        in_specs=vmem(4),
+        out_specs=vmem(1)[0],
+    )(hidden_rows[0], query, send_counts, row_session[0].T)
     msg = swap(msg, "inst")
 
     cache = pl.pallas_call(
@@ -303,7 +288,7 @@
         in_specs=vmem(2),
         out_specs=vmem(1)[0],
         scratch_shapes=[pltpu.VMEM((128, wide), bf16)],
-    )(*near(msg), kv_weight)
+    )(*near(msg), weight)
     qx = swap(swap(qw, "inst"), "head")
 
     part, code = pl.pallas_call(
@@ -330,20 +315,26 @@
 
     y = pl.pallas_call(
         mix_body,
-        out_shape=pltpu.VMEM((blocks, ROWS, 512), bf16),
+        out_shape=pltpu.VMEM((insts, ROWS, 256), bf16),
         in_specs=vmem(3),
         out_specs=vmem(1)[0],
     )(*near(prob, code, msg))
-    y = swap(y, "head")
+    y = swap(swap(y, "head"), "inst")
+
+    out = pl.pallas_call(
+        value_body,
+        out_shape=pltpu.VMEM((insts, ROWS, HDIM), f32),
+        in_specs=vmem(2),
+        out_specs=vmem(1)[0],
+    )(*near(y), weight)
+    out = swap(out, "inst")
 
     return pl.pallas_call(
         last_body,
         out_shape=jax.ShapeDtypeStruct((SESS, wide), bf16),
-        in_specs=[vmem(1)[0], pl.BlockSpec(memory_space=pl.ANY), vmem(1)[0]],
-        out_specs=vmem(1)[0],
-        scratch_shapes=[pltpu.VMEM(values.shape, bf16), pltpu.SemaphoreType.DMA((8,))],
-        compiler_params=pltpu.CompilerParams(vmem_limit_bytes=56 * 2**20),
-    )(*near(y), values, *near(base))
+        in_specs=vmem(2),
+        out_specs=vmem(1)[0],
+    )(*near(out, base))
 
 
 def solution(mesh):

time: 126 us -> 132 us (1.048)
  blocking collectives: 90.7 us -> 114 us
  between operations: 13.4 us -> 0.05 us
  Pallas kernels: 11.9 us -> 6.96 us
    all_to_all x5 -> x7, blocking collectives: 90.7 us -> 114 us  [local(): lax.all_to_all(t, axis, split_axis=0, concat_axis=0, tiled=True)]
    pallas_call x1, Pallas kernels: 3.98 us -> 0.6 us  [local(): pl.pallas_call(last_body, out_shape=jax.ShapeDtypeStruct((SESS, wide), bf...]
    pallas_call x2 -> x3, Pallas kernels: 2.66 us -> 2.14 us  [the longest x1 1.44 us: local(): pl.pallas_call(pack_body, out_shape=pltpu.VMEM((insts, cap, width), bf16)...]
  transfers between devices with their start and end apart: 2 -> 1, of which waited for: 1 -> 1; matrix products, arithmetic and copies ran while one was open for 0% -> 0% of each run, Pallas kernels for 5% -> 2%
where the time goes in v7:
time: 132 us; the launch traced here: 131 us
  blocking collectives  114 us (86%)
  Pallas kernels  6.96 us (5%)
  waiting for transfers between devices  6.4 us (5%)
  starting transfers between devices  3.41 us (3%)
    all_to_all x7, blocking collectives, local(): lax.all_to_all(t, axis, split_axis=0, concat_axis=0, tiled=True)  114 us
    all_to_all x1, waiting for transfers between devices, local(): lax.all_to_all(t, axis, split_axis=0, concat_axis=0, tiled=True)  6.4 us
    all_to_all x1, starting transfers between devices, local(): lax.all_to_all(t, axis, split_axis=0, concat_axis=0, tiled=True)  3.41 us
  transfers between devices with their start and end apart: 1, of which 1 were waited for; matrix products, arithmetic and copies ran while one was open for 0% of the time, Pallas kernels for 2%

profile of v7, /device:TPU:1, one launch (start us, length us, event | category | flops | bytes accessed | tf_op | source)
XLA Modules:
  0.0 131.1 jit_solution(10989996520107271793)
XLA Ops:
  0.0 0.0 copy-start
  0.0 1.4 %shard_map.100 = bf16[32,16,640]{2,1,0:T(8,128)(2,1)S(1)} custom-call(bf16[32,16,576]{2,1,0:T(8,128)(2,1)} %bitcast.4, bf16[2,384]{1,0:T(2,128)(2,1)} %q_ref.3, s32[1,32]{1,0:T(1,128)} %counts_ref.1, s32[16,32]{1,0:T(8,128)} %bitcast.5), custom_call_target="tpu_custom_call" | custom-call | tf_op jit(solution)/shard_map/pallas_call | solution.py:267
  1.4 29.9 %all_to_all.40.msg_ref = bf16[32,16,640]{2,1,0:T(8,128)(2,1)S(1)} all-to-all(bf16[32,16,640]{2,1,0:T(8,128)(2,1)S(1)} %shard_map.100), channel_id=1, replica_groups=mesh['inst'=32,'head'=16] {'inst'}, dimensions={0} | all-to-all | bytes 1310720 | tf_op jit(solution)/shard_map/all_to_all | solution.py:263
  31.3 0.0 copy-done
  31.3 0.7 shard_map.101
  32.1 17.4 %all_to_all.41 = bf16[32,8,256]{2,1,0:T(8,128)(2,1)S(1)} all-to-all(bf16[32,8,256]{2,1,0:T(8,128)(2,1)S(1)} %shard_map.101), channel_id=1, replica_groups=mesh['inst'=32,'head'=16] {'inst'}, dimensions={0} | all-to-all | bytes 262144 | tf_op jit(solution)/shard_map/all_to_all | solution.py:263
  49.4 18.8 %all_to_all.42.qx_ref = bf16[32,8,256]{2,1,0:T(8,128)(2,1)S(1)} all-to-all(bf16[32,8,256]{2,1,0:T(8,128)(2,1)S(1)} %all_to_all.41), channel_id=1, replica_groups=mesh['inst'=32,'head'=16] {'head'}, dimensions={0} | all-to-all | bytes 262144 | tf_op jit(solution)/shard_map/all_to_all | solution.py:263
  68.2 1.0 shard_map.102
  69.2 3.4 %all-to-all-start.3 = ((f32[16,4,512]{2,1,0:T(4,128)}), f32[16,4,512]{2,1,0:T(4,128)S(1)}, u32[]{:S(2)}, u32[]{:S(2)}) async-start(f32[16,4,512]{2,1,0:T(4,128)} %get-tuple-element.9), calls=%async_computation.3 | async-start | bytes 262144 | tf_op jit(solution)/shard_map/all_to_all | solution.py:263
  72.6 2.1 %shard_map.103.cache_ref = f32[3,8,128]{2,1,0:T(8,128)S(1)} custom-call(s32[2]{0:T(128)} %lengths_ref.1, bf16[2,384]{1,0:T(2,128)(2,1)} %q_ref.3, bf16[2,384]{1,0:T(2,128)(2,1)} %nk_ref.1, bf16[2,384]{1,0:T(2,128)(2,1)} %nv_ref.1, bf16[2,1024,384]{2,1,0:T(8,128)(2,1)} %key_ref.1, bf16[2,1024,384]{2,1,0:T(8,128)(2,1)} %value_ref.1), custom_call_target="tpu_custom_call" | custom-call | tf_op jit(solution)/shard_map/pallas_call | solution.py:275
  74.7 6.4 %all-to-all-done.3.parts_ref = f32[16,4,512]{2,1,0:T(4,128)S(1)} async-done(((f32[16,4,512]{2,1,0:T(4,128)}), f32[16,4,512]{2,1,0:T(4,128)S(1)}, u32[]{:S(2)}, u32[]{:S(2)}) %all-to-all-start.3) | async-done | bytes 131104 | tf_op jit(solution)/shard_map/all_to_all | solution.py:263
  81.1 0.4 shard_map.104
  81.5 10.5 %all_to_all.43.prob_ref = bf16[16,4,512]{2,1,0:T(4,128)(2,1)S(1)} all-to-all(bf16[16,4,512]{2,1,0:T(4,128)(2,1)S(1)} %get-tuple-element.11), channel_id=1, replica_groups=mesh['inst'=32,'head'=16] {'head'}, dimensions={0} | all-to-all | bytes 131072 | tf_op jit(solution)/shard_map/all_to_all | solution.py:263
  92.0 0.5 shard_map.105
  92.5 11.8 %all_to_all.44 = bf16[32,8,256]{2,1,0:T(8,128)(2,1)S(1)} all-to-all(bf16[32,8,256]{2,1,0:T(8,128)(2,1)S(1)} %shard_map.105), channel_id=1, replica_groups=mesh['inst'=32,'head'=16] {'head'}, dimensions={0} | all-to-all | bytes 262144 | tf_op jit(solution)/shard_map/all_to_all | solution.py:263
  104.3 12.5 %all_to_all.45.y_ref = bf16[32,8,256]{2,1,0:T(8,128)(2,1)S(1)} all-to-all(bf16[32,8,256]{2,1,0:T(8,128)(2,1)S(1)} %all_to_all.44), channel_id=1, replica_groups=mesh['inst'=32,'head'=16] {'inst'}, dimensions={0} | all-to-all | bytes 262144 | tf_op jit(solution)/shard_map/all_to_all | solution.py:263
  116.8 0.2 shard_map.106
  117.0 13.5 %all_to_all.46.parts_ref = f32[32,8,128]{2,1,0:T(8,128)S(1)} all-to-all(f32[32,8,128]{2,1,0:T(8,128)S(1)} %shard_map.106), channel_id=1, replica_groups=mesh['inst'=32,'head'=16] {'inst'}, dimensions={0} | all-to-all | bytes 262144 | tf_op jit(solution)/shard_map/all_to_all | solution.py:263
  130.5 0.6 shard_map.107
Async XLA Ops:
  0.0 31.3 %copy-start = (bf16[288,768]{1,0:T(8,128)(2,1)S(1)}, bf16[288,768]{1,0:T(8,128)(2,1)}, u32[]{:S(2)}) copy-start(bf16[288,768]{1,0:T(8,128)(2,1)} %w_ref.3) | copy-start | bytes 1327108
  69.2 11.9 %all-to-all-start.3 = ((f32[16,4,512]{2,1,0:T(4,128)}), f32[16,4,512]{2,1,0:T(4,128)S(1)}, u32[]{:S(2)}, u32[]{:S(2)}) async-start(f32[16,4,512]{2,1,0:T(4,128)} %get-tuple-element.9), calls=%async_computation.3 | async-start | bytes 262144 | tf_op jit(solution)/shard_map/all_to_all | solution.py:263

commit v8 on v6

--- a/solution.py
+++ b/solution.py
@@ -303,7 +303,7 @@
         in_specs=vmem(2),
         out_specs=vmem(1)[0],
         scratch_shapes=[pltpu.VMEM((128, wide), bf16)],
-    )(*near(msg), kv_weight)
+    )(*near(msg, kv_weight))
     qx = swap(swap(qw, "inst"), "head")
 
     part, code = pl.pallas_call(

time: 126 us -> 126 us (level)
  transfers between devices with their start and end apart: 2 -> 2, of which waited for: 1 -> 2; matrix products, arithmetic and copies ran while one was open for 0% -> 0% of each run, Pallas kernels for 5% -> 4%
where the time goes in v8:
time: 126 us
  blocking collectives  90.7 us (72%)
  between operations  13.4 us (11%)
  Pallas kernels  11 us (9%)
  waiting for transfers between devices  7.53 us (6%)
  starting transfers between devices  3.41 us (3%)
    all_to_all x5, blocking collectives, local(): lax.all_to_all(t, axis, split_axis=0, concat_axis=0, tiled=True)  90.7 us
    all_to_all x1, waiting for transfers between devices, local(): lax.all_to_all(t, axis, split_axis=0, concat_axis=0, tiled=True)  6.37 us
    pallas_call x1, Pallas kernels, local(): pl.pallas_call(last_body, out_shape=jax.ShapeDtypeStruct((SESS, wide), bf...  3.98 us
    all_to_all x1, starting transfers between devices, local(): lax.all_to_all(t, axis, split_axis=0, concat_axis=0, tiled=True)  3.41 us
  transfers between devices with their start and end apart: 2, of which 2 were waited for; matrix products, arithmetic and copies ran while one was open for 0% of the time, Pallas kernels for 4%

profile of v8, /device:TPU:1, one launch (start us, length us, event | category | flops | bytes accessed | tf_op | source)
XLA Modules:
  0.0 126.0 jit_solution(2355628521051353072)
XLA Ops:
  6.5 0.0 copy-start
  6.5 0.0 all-gather.2.cloned.1.call-start
  6.5 2.3 %shard_map.100 = (bf16[32,16,640]{2,1,0:T(8,128)(2,1)S(1)}, bf16[288,384]{1,0:T(8,128)(2,1)}) custom-call(bf16[32,16,576]{2,1,0:T(8,128)(2,1)} %bitcast.4, bf16[2,384]{1,0:T(2,128)(2,1)} %q_ref.3, s32[1,32]{1,0:T(1,128)} %counts_ref.1, s32[16,32]{1,0:T(8,128)} %bitcast.5, bf16[288,768]{1,0:T(8,128)(2,1)} %w_ref.3), custom_call_target="tpu_custom_call" | custom-call | tf_op jit(solution)/shard_map/pallas_call | solution.py:278
  8.8 0.0 all-gather.2.cloned.1.call-update
  8.8 29.9 %all_to_all.30.msg_ref = bf16[32,16,640]{2,1,0:T(8,128)(2,1)S(1)} all-to-all(bf16[32,16,640]{2,1,0:T(8,128)(2,1)S(1)} %get-tuple-element.11), channel_id=1, replica_groups=mesh['inst'=32,'head'=16] {'inst'}, dimensions={0} | all-to-all | bytes 1310720 | tf_op jit(solution)/shard_map/all_to_all | solution.py:276
  38.8 0.0 copy-done
  38.8 0.7 shard_map.101
  39.5 20.1 %all_to_all.31 = bf16[32,8,256]{2,1,0:T(8,128)(2,1)S(1)} all-to-all(bf16[32,8,256]{2,1,0:T(8,128)(2,1)S(1)} %shard_map.101), channel_id=1, replica_groups=mesh['inst'=32,'head'=16] {'inst'}, dimensions={0} | all-to-all | bytes 262144 | tf_op jit(solution)/shard_map/all_to_all | solution.py:276
  59.6 18.3 %all_to_all.32.qx_ref = bf16[32,8,256]{2,1,0:T(8,128)(2,1)S(1)} all-to-all(bf16[32,8,256]{2,1,0:T(8,128)(2,1)S(1)} %all_to_all.31), channel_id=1, replica_groups=mesh['inst'=32,'head'=16] {'head'}, dimensions={0} | all-to-all | bytes 262144 | tf_op jit(solution)/shard_map/all_to_all | solution.py:276
  77.9 1.0 shard_map.102
  79.0 3.4 %all-to-all-start.3 = ((f32[16,4,512]{2,1,0:T(4,128)}), f32[16,4,512]{2,1,0:T(4,128)S(1)}, u32[]{:S(2)}, u32[]{:S(2)}) async-start(f32[16,4,512]{2,1,0:T(4,128)} %get-tuple-element.12), calls=%async_computation.3 | async-start | bytes 262144 | tf_op jit(solution)/shard_map/all_to_all | solution.py:276
  82.4 2.1 %shard_map.103.cache_ref = f32[3,8,128]{2,1,0:T(8,128)S(1)} custom-call(s32[2]{0:T(128)} %lengths_ref.1, bf16[2,384]{1,0:T(2,128)(2,1)} %q_ref.3, bf16[2,384]{1,0:T(2,128)(2,1)} %nk_ref.1, bf16[2,384]{1,0:T(2,128)(2,1)} %nv_ref.1, bf16[2,1024,384]{2,1,0:T(8,128)(2,1)} %key_ref.1, bf16[2,1024,384]{2,1,0:T(8,128)(2,1)} %value_ref.1), custom_call_target="tpu_custom_call" | custom-call | tf_op jit(solution)/shard_map/pallas_call | solution.py:290
  84.5 6.4 %all-to-all-done.3.parts_ref = f32[16,4,512]{2,1,0:T(4,128)S(1)} async-done(((f32[16,4,512]{2,1,0:T(4,128)}), f32[16,4,512]{2,1,0:T(4,128)S(1)}, u32[]{:S(2)}, u32[]{:S(2)}) %all-to-all-start.3) | async-done | bytes 131104 | tf_op jit(solution)/shard_map/all_to_all | solution.py:276
  90.9 0.4 shard_map.104
  91.3 10.5 %all_to_all.33.prob_ref = bf16[16,4,512]{2,1,0:T(4,128)(2,1)S(1)} all-to-all(bf16[16,4,512]{2,1,0:T(4,128)(2,1)S(1)} %get-tuple-element.14), channel_id=1, replica_groups=mesh['inst'=32,'head'=16] {'head'}, dimensions={0} | all-to-all | bytes 131072 | tf_op jit(solution)/shard_map/all_to_all | solution.py:276
  101.8 0.5 shard_map.105
  102.3 11.8 %all_to_all.34.y_ref = bf16[16,8,512]{2,1,0:T(8,128)(2,1)S(1)} all-to-all(bf16[16,8,512]{2,1,0:T(8,128)(2,1)S(1)} %shard_map.105), channel_id=1, replica_groups=mesh['inst'=32,'head'=16] {'head'}, dimensions={0} | all-to-all | bytes 262144 | tf_op jit(solution)/shard_map/all_to_all | solution.py:276
  114.0 1.1 all-gather.2.cloned.1.call-done.w_ref
  115.2 4.0 %shard_map.106 = bf16[2,384]{1,0:T(2,128)(2,1)} custom-call(bf16[16,8,512]{2,1,0:T(8,128)(2,1)S(1)} %all_to_all.34.y_ref, bf16[9216,384]{1,0:T(8,128)(2,1)} %all-gather.2.cloned.1.call-done.w_ref, f32[8,128]{1,0:T(8,128)S(1)} %get-tuple-element.16.base_ref), custom_call_target="tpu_custom_call" | custom-call | tf_op jit(solution)/shard_map/pallas_call | solution.py:339
Async XLA Ops:
  6.5 32.2 %copy-start = (bf16[288,768]{1,0:T(8,128)(2,1)S(1)}, bf16[288,768]{1,0:T(8,128)(2,1)}, u32[]{:S(2)}) copy-start(bf16[288,768]{1,0:T(8,128)(2,1)} %w_ref.3) | copy-start | bytes 1327108
  6.5 108.6 %all-gather.2.cloned.1.call-start = ((), (), s32[]{:S(2)}) async-start(), calls=%async_computation.6 | async-start | bytes 7299072 | tf_op jit(solution)/shard_map/all_gather | solution.py:287
  79.0 11.9 %all-to-all-start.3 = ((f32[16,4,512]{2,1,0:T(4,128)}), f32[16,4,512]{2,1,0:T(4,128)S(1)}, u32[]{:S(2)}, u32[]{:S(2)}) async-start(f32[16,4,512]{2,1,0:T(4,128)} %get-tuple-element.12), calls=%async_computation.3 | async-start | bytes 262144 | tf_op jit(solution)/shard_map/all_to_all | solution.py:276
Sparse Core Ops, SparseCore 0:
  10.5 104.6 all-gather.1

commit v9 on v8

--- a/solution.py
+++ b/solution.py
@@ -70,7 +70,7 @@
         out_ref[i, :, 512:640] = t.astype(bf16)
 
 
-def qw_body(msg_ref, w_ref, out_ref, odd_ref):
+def qw_body(msg_ref, w_ref, _, out_ref, odd_ref):
     sources, cap, width = msg_ref.shape
     heads = w_ref.shape[1] // (2 * HDIM)
     wide = heads * HDIM
@@ -300,10 +300,10 @@
     qw = pl.pallas_call(
         qw_body,
         out_shape=pltpu.VMEM((insts, ROWS, 256), bf16),
-        in_specs=vmem(2),
+        in_specs=vmem(3),
         out_specs=vmem(1)[0],
         scratch_shapes=[pltpu.VMEM((128, wide), bf16)],
-    )(*near(msg, kv_weight))
+    )(*near(msg, kv_weight, cache))
     qx = swap(swap(qw, "inst"), "head")
 
     part, code = pl.pallas_call(

time: 126 us -> 126 us (level)
  blocking collectives: 90.7 us -> 72.7 us
  starting transfers between devices: 3.41 us -> 13.7 us
  waiting for transfers between devices: 7.53 us -> 15.7 us
    all_to_all x5, blocking collectives: 90.7 us -> 72.7 us  [local(): lax.all_to_all(t, axis, split_axis=0, concat_axis=0, tiled=True)]
    all_to_all x1, starting transfers between devices: 3.41 us -> 13.7 us  [local(): lax.all_to_all(t, axis, split_axis=0, concat_axis=0, tiled=True)]
    all_to_all x1, waiting for transfers between devices: 6.37 us -> 14.2 us  [local(): lax.all_to_all(t, axis, split_axis=0, concat_axis=0, tiled=True)]
  transfers between devices with their start and end apart: 2 -> 2, of which waited for: 2 -> 2; matrix products, arithmetic and copies ran while one was open for 0% -> 0% of each run, Pallas kernels for 4% -> 3%
where the time goes in v9:
time: 126 us
  blocking collectives  72.7 us (58%)
  waiting for transfers between devices  15.7 us (12%)
  starting transfers between devices  13.7 us (11%)
  between operations  13.4 us (11%)
  Pallas kernels  10.5 us (8%)
    all_to_all x5, blocking collectives, local(): lax.all_to_all(t, axis, split_axis=0, concat_axis=0, tiled=True)  72.7 us
    all_to_all x1, waiting for transfers between devices, local(): lax.all_to_all(t, axis, split_axis=0, concat_axis=0, tiled=True)  14.2 us
    all_to_all x1, starting transfers between devices, local(): lax.all_to_all(t, axis, split_axis=0, concat_axis=0, tiled=True)  13.7 us
    pallas_call x1, Pallas kernels, local(): pl.pallas_call(last_body, out_shape=jax.ShapeDtypeStruct((SESS, wide), bf...  3.98 us
  transfers between devices with their start and end apart: 2, of which 2 were waited for; matrix products, arithmetic and copies ran while one was open for 0% of the time, Pallas kernels for 3%

profile of v9, /device:TPU:1, one launch (start us, length us, event | category | flops | bytes accessed | tf_op | source)
XLA Modules:
  0.0 126.0 jit_solution(4402088807553197322)
XLA Ops:
  6.5 0.0 all-gather.2.cloned.1.call-start
  6.5 2.4 %shard_map.100 = (bf16[32,16,640]{2,1,0:T(8,128)(2,1)}, bf16[288,384]{1,0:T(8,128)(2,1)}) custom-call(bf16[32,16,576]{2,1,0:T(8,128)(2,1)} %bitcast.4, bf16[2,384]{1,0:T(2,128)(2,1)} %q_ref.3, s32[1,32]{1,0:T(1,128)} %counts_ref.1, s32[16,32]{1,0:T(8,128)} %bitcast.5, bf16[288,768]{1,0:T(8,128)(2,1)} %w_ref.3), custom_call_target="tpu_custom_call" | custom-call | tf_op jit(solution)/shard_map/pallas_call | solution.py:278
  9.0 0.0 all-gather.2.cloned.1.call-update
  9.0 13.7 %all-to-all-start = ((bf16[32,16,640]{2,1,0:T(8,128)(2,1)}), bf16[32,16,640]{2,1,0:T(8,128)(2,1)S(1)}, u32[]{:S(2)}, u32[]{:S(2)}) async-start(bf16[32,16,640]{2,1,0:T(8,128)(2,1)} %get-tuple-element.11), calls=%async_computation | async-start | bytes 1310720 | tf_op jit(solution)/shard_map/all_to_all | solution.py:276
  22.7 0.0 copy-start
  22.7 2.1 %shard_map.101._.cache_ref = f32[3,8,128]{2,1,0:T(8,128)S(1)} custom-call(s32[2]{0:T(128)} %lengths_ref.1, bf16[2,384]{1,0:T(2,128)(2,1)} %q_ref.3, bf16[2,384]{1,0:T(2,128)(2,1)} %nk_ref.1, bf16[2,384]{1,0:T(2,128)(2,1)} %nv_ref.1, bf16[2,1024,384]{2,1,0:T(8,128)(2,1)} %key_ref.1, bf16[2,1024,384]{2,1,0:T(8,128)(2,1)} %value_ref.1), custom_call_target="tpu_custom_call" | custom-call | tf_op jit(solution)/shard_map/pallas_call | solution.py:290
  24.9 14.2 %all-to-all-done.msg_ref = bf16[32,16,640]{2,1,0:T(8,128)(2,1)S(1)} async-done(((bf16[32,16,640]{2,1,0:T(8,128)(2,1)}), bf16[32,16,640]{2,1,0:T(8,128)(2,1)S(1)}, u32[]{:S(2)}, u32[]{:S(2)}) %all-to-all-start) | async-done | bytes 655392 | tf_op jit(solution)/shard_map/all_to_all | solution.py:276
  39.1 0.0 copy-done
  39.1 0.7 shard_map.102
  39.8 20.3 %all_to_all.30 = bf16[32,8,256]{2,1,0:T(8,128)(2,1)S(1)} all-to-all(bf16[32,8,256]{2,1,0:T(8,128)(2,1)S(1)} %shard_map.102), channel_id=1, replica_groups=mesh['inst'=32,'head'=16] {'inst'}, dimensions={0} | all-to-all | bytes 262144 | tf_op jit(solution)/shard_map/all_to_all | solution.py:276
  60.2 18.8 %all_to_all.31.qx_ref = bf16[32,8,256]{2,1,0:T(8,128)(2,1)S(1)} all-to-all(bf16[32,8,256]{2,1,0:T(8,128)(2,1)S(1)} %all_to_all.30), channel_id=1, replica_groups=mesh['inst'=32,'head'=16] {'head'}, dimensions={0} | all-to-all | bytes 262144 | tf_op jit(solution)/shard_map/all_to_all | solution.py:276
  78.9 0.4 shard_map.103
  79.3 11.6 %all_to_all.32.parts_ref = f32[16,4,512]{2,1,0:T(4,128)S(1)} all-to-all(f32[16,4,512]{2,1,0:T(4,128)S(1)} %get-tuple-element.12), channel_id=1, replica_groups=mesh['inst'=32,'head'=16] {'head'}, dimensions={0} | all-to-all | bytes 262144 | tf_op jit(solution)/shard_map/all_to_all | solution.py:276
  90.9 0.4 shard_map.104
  91.3 10.2 %all_to_all.33.prob_ref = bf16[16,4,512]{2,1,0:T(4,128)(2,1)S(1)} all-to-all(bf16[16,4,512]{2,1,0:T(4,128)(2,1)S(1)} %get-tuple-element.14), channel_id=1, replica_groups=mesh['inst'=32,'head'=16] {'head'}, dimensions={0} | all-to-all | bytes 131072 | tf_op jit(solution)/shard_map/all_to_all | solution.py:276
  101.5 0.5 shard_map.105
  102.0 11.8 %all_to_all.34.y_ref = bf16[16,8,512]{2,1,0:T(8,128)(2,1)S(1)} all-to-all(bf16[16,8,512]{2,1,0:T(8,128)(2,1)S(1)} %shard_map.105), channel_id=1, replica_groups=mesh['inst'=32,'head'=16] {'head'}, dimensions={0} | all-to-all | bytes 262144 | tf_op jit(solution)/shard_map/all_to_all | solution.py:276
  113.8 1.4 %all-gather.2.cloned.1.call-done.w_ref = bf16[9216,384]{1,0:T(8,128)(2,1)} async-done(((bf16[288,384]{1,0:T(8,128)(2,1)}), bf16[9216,384]{1,0:T(8,128)(2,1)}) %all-gather.2.cloned.1.call-update) | async-done | bytes 7077904 | tf_op jit(solution)/shard_map/all_gather | solution.py:287
  115.2 4.0 %shard_map.106 = bf16[2,384]{1,0:T(2,128)(2,1)} custom-call(bf16[16,8,512]{2,1,0:T(8,128)(2,1)S(1)} %all_to_all.34.y_ref, bf16[9216,384]{1,0:T(8,128)(2,1)} %all-gather.2.cloned.1.call-done.w_ref, f32[8,128]{1,0:T(8,128)S(1)} %get-tuple-element.16.base_ref), custom_call_target="tpu_custom_call" | custom-call | tf_op jit(solution)/shard_map/pallas_call | solution.py:339
Async XLA Ops:
  6.5 108.7 %all-gather.2.cloned.1.call-start = ((), (), s32[]{:S(2)}) async-start(), calls=%async_computation.6 | async-start | bytes 7299072 | tf_op jit(solution)/shard_map/all_gather | solution.py:287
  9.0 30.1 %all-to-all-start = ((bf16[32,16,640]{2,1,0:T(8,128)(2,1)}), bf16[32,16,640]{2,1,0:T(8,128)(2,1)S(1)}, u32[]{:S(2)}, u32[]{:S(2)}) async-start(bf16[32,16,640]{2,1,0:T(8,128)(2,1)} %get-tuple-element.11), calls=%async_computation | async-start | bytes 1310720 | tf_op jit(solution)/shard_map/all_to_all | solution.py:276
  22.7 16.4 %copy-start = (bf16[288,768]{1,0:T(8,128)(2,1)S(1)}, bf16[288,768]{1,0:T(8,128)(2,1)}, u32[]{:S(2)}) copy-start(bf16[288,768]{1,0:T(8,128)(2,1)} %w_ref.3) | copy-start | bytes 1327108
Sparse Core Ops, SparseCore 0:
  10.5 104.6 all-gather.1
